TPU v7x, 256 devices: a whole 4x4x8 slice. The times are simulated.
256 devices in a mesh: wide: 32 (over z_lo, y, core), narrow: 8 (over x, z_hi).
Axes of the slice: x: 4, y: 4, z: 8 (z_hi: 2, z_lo: 4; z = z_hi * 4 + z_lo), core: 2. Of those that a mesh axis runs over, the one named last changes fastest.
Arguments:
- amplitudes: float32 [2, 67108864], P(None, ('wide', 'narrow')), may hold values from -6 to 6
- joined_gates: float32 [4, 2, 128, 128], replicated, may hold values from -0.4 to 0.4
- qubit_order: int32 [4, 8], replicated, may hold values from 0 to 7, each once within a row
- global_gates: float32 [4, 2, 2, 2], replicated, may hold values from -3 to 3
Outputs:
- final_state: float32 [2, 67108864], P(None, ('wide', 'narrow'))
Inputs may be any that keep to these rules, and one draw needn't show every extreme that they name: Each row of qubit_order is a permutation of 0 to 7.
All inputs are finite; a program needn't handle non-finite values.
Results may differ from a plain program's by a relative error of at most 0.0001.
Values sent between devices are 32-bit elements; how exact they have to be, the bound alone decides.
A program may use at most 64 MiB of HBM per device.

v0:
```python
import functools

import jax
import jax.numpy as jnp
from jax import lax
from jax.sharding import PartitionSpec as P
import jax.experimental.pallas as pl
import jax.experimental.pallas.tpu as pltpu

MESH = pl.DeviceIdType.MESH
LANES = 128
BLOCK = 512

UNITS = ((1, 0), (3, 0), (2, 0), (0, 0))
ORDER = (
    ("m", -1), ("a1", 0), ("b1", 0), ("a1", 1), ("b1", 1), ("a1", 2), ("b1", 2), ("a2", 0), ("a1", 3),
    ("b1", 3), ("b2", 0), ("a2", 1), ("b2", 1), ("a3", 0), ("b2", 2), ("a2", 2), ("b2", 3), ("a3", 1),
    ("a2", 3), ("a3", 2), ("a4", 0), ("a3", 3), ("bz", 0), ("a5", 0), ("a4", 1), ("a6", 0), ("a4", 2),
    ("b4", 0), ("a5", 1), ("bz", 1), ("a7", 0), ("a5", 2), ("a4", 3), ("a6", 1), ("a6", 2), ("a8", 0),
    ("bz", 2), ("b4", 1), ("a5", 3), ("a7", 1), ("a7", 2), ("bz", 3), ("a6", 3), ("a8", 1), ("b4", 2),
    ("b4", 3), ("a7", 3), ("a8", 2),
)


SUBS = len(UNITS) // 4
U = len(UNITS)
R = BLOCK // SUBS
H = R // 2
Q = R // 8
NQ = Q // 4


def flip(value, mask, bits):
    total = 0
    for bit in range(bits):
        step = 2**bit
        total = total + lax.rem(lax.div(value, step) + (mask // step) % 2, 2) * step
    return total


def cmul_add(first, x, second, y):
    real = first[0] * x[0] - first[1] * x[1] + (second[0] * y[0] - second[1] * y[1])
    imag = first[0] * x[1] + first[1] * x[0] + (second[0] * y[1] + second[1] * y[0])
    return real, imag


def coefs(gates, layer, row, col):
    return gates[layer, 0, row, col], gates[layer, 1, row, col]


def exact_dot(a, b, dims):
    return lax.dot_general(
        a, b, (dims, ((), ())), precision=lax.Precision.HIGHEST, preferred_element_type=jnp.float32
    )


def build_local(joined, order, total, high, low):
    layers = joined.shape[0]
    rows = lax.broadcasted_iota(jnp.int32, (256, 256), 0)
    cols = lax.broadcasted_iota(jnp.int32, (256, 256), 1)
    eye = (rows == cols).astype(jnp.float32)
    total[pl.ds(0, 256), :] = eye
    total[pl.ds(256, 256), :] = jnp.zeros((256, 256), jnp.float32)
    for layer in range(layers):
        parts = []
        for half in range(2):
            old = total[:, pl.ds(half * LANES, LANES)]
            by_real = exact_dot(old, joined[layer, 0], ((1,), (1,)))
            by_imag = exact_dot(old, joined[layer, 1], ((1,), (1,)))
            real = by_real[:256] - by_imag[256:]
            imag = by_imag[:256] + by_real[256:]
            parts.append(jnp.concatenate([real, imag], axis=0))
        mixed = jnp.concatenate(parts, axis=1)
        source = jnp.zeros((256, 256), jnp.int32)
        for qubit in range(8):
            bit = jnp.bitwise_and(jnp.right_shift(cols, qubit), 1)
            source = source + jnp.left_shift(bit, order[layer, qubit])
        picker = (rows == source).astype(jnp.float32)
        total[...] = exact_dot(mixed, picker, ((1,), (0,)))
    for half in range(2):
        for half_out in range(2):
            real = total[pl.ds(half * LANES, LANES), pl.ds(half_out * LANES, LANES)]
            imag = total[pl.ds(256 + half * LANES, LANES), pl.ds(half_out * LANES, LANES)]
            for part, part_out, block in ((0, 0, real), (0, 1, imag), (1, 0, -imag), (1, 1, real)):
                at = pl.ds((half * 2 + part) * LANES, LANES), pl.ds((half_out * 2 + part_out) * LANES, LANES)
                top = block.astype(jnp.bfloat16)
                high[at] = top
                low[at] = (block - top.astype(jnp.float32)).astype(jnp.bfloat16)


def group_step(slots, sent, gates, parities, high, low):
    planes = [None] * 4
    for half in range(2):
        values = []
        for m in range(8):
            values.append(tuple(slots[m, pl.ds(2 * half + part, NQ, stride=4), :] for part in range(2)))
        for bit in range(3):
            own = parities[bit]
            other = 1 - own
            g_oo, g_ox = coefs(gates, bit, own, own), coefs(gates, bit, own, other)
            g_xx, g_xo = coefs(gates, bit, other, other), coefs(gates, bit, other, own)
            fresh = list(values)
            for m in range(8):
                if not m >> bit & 1:
                    x0, x1 = values[m], values[m | 1 << bit]
                    fresh[m] = cmul_add(g_oo, x0, g_ox, x1)
                    fresh[m | 1 << bit] = cmul_add(g_xx, x1, g_xo, x0)
            values = fresh
        for part in range(2):
            planes[2 * half + part] = jnp.concatenate([v[part] for v in values], axis=0)
    block = jnp.concatenate(planes, axis=1)
    top = block.astype(jnp.bfloat16)
    rest = (block - top.astype(jnp.float32)).astype(jnp.bfloat16)
    dot = functools.partial(jnp.dot, preferred_element_type=jnp.float32)
    result = dot(top, high[...]) + (dot(rest, high[...]) + dot(top, low[...]))
    for m in range(8):
        for k in range(4):
            sent[m, pl.ds(k, NQ, stride=4), :] = result[m * NQ : (m + 1) * NQ, k * LANES : (k + 1) * LANES]


def kernel(
    x_ref, joined_hbm, order_ref, gates, out_ref,
    joined, total, high, low,
    ao, z1, g1, f1, f2, f3, an, ya, sa, ta, oa, yb, sb, tb, ob, zb, rb,
    jsem, aosem, outsem,
    z1s, z1r, f1s, f1r, f2s, f2r, f3s, f3r, f4s, f4r,
    yas, yar, tas, tar, oas, oar, ybs, ybr, tbs, tbr, obs, obr, zbs, zbr,
):
    w, n = lax.axis_index("wide"), lax.axis_index("narrow")
    p, q, s = lax.div(w, 16), lax.rem(lax.div(w, 8), 2), lax.rem(w, 8)
    x, zh = lax.div(n, 2), lax.rem(n, 2)
    parities = [lax.rem(lax.div(s, 2**bit), 2) for bit in range(3)]
    pair = (p * 16 + (1 - q) * 8 + s, n)
    same = 1 - lax.rem(p + q, 2)
    beyond = ((1 - p) * 16 + (1 - q) * 8 + s, x * 2 + lax.rem(zh + same, 2))
    others = [flip(s, m, 3) for m in range(8)]
    group = [(p * 16 + q * 8 + others[m], n) for m in range(8)]
    across = [(w, flip(x, u, 2) * 2 + zh) for u in range(4)]
    aligned = lambda rows: pl.multiple_of(rows, 8)
    at_a = [aligned((flip(x, u, 2) * 2 + 1 - zh) * BLOCK + sub * R) for u, sub in UNITS]
    at_b = [aligned((flip(x, u, 2) * 2 + zh) * BLOCK + sub * R) for u, sub in UNITS]
    low_half, high_half = aligned(q * H), aligned((1 - q) * H)
    mine = aligned(s * Q)

    barrier = pltpu.get_barrier_semaphore()
    partners = [pair, beyond] + group[1:] + across[1:]
    for there in partners:
        pl.semaphore_signal(barrier, inc=1, device_id=there, device_id_type=MESH)

    pltpu.make_async_copy(joined_hbm, joined, jsem).start()
    for i in range(U):
        pltpu.make_async_copy(x_ref.at[pl.ds(aligned(at_a[i] + (1 - q) * H), H)], ao.at[i], aosem.at[i]).start()
    pl.semaphore_wait(barrier, len(partners))

    def remote(src, dst, send_sem, recv_sem, there):
        return pltpu.make_async_remote_copy(
            src_ref=src, dst_ref=dst, send_sem=send_sem, recv_sem=recv_sem, device_id=there, device_id_type=MESH
        )

    def wait_for(ref, sem):
        pltpu.make_async_copy(ref, ref, sem).wait()

    def exchange(source, base, slots, send_sem, recv_sem):
        for m in range(8):
            src = source.at[pl.ds(aligned(base + others[m] * Q), Q)]
            if m:
                remote(src, slots.at[m], send_sem, recv_sem, group[m]).start()
            else:
                pltpu.make_async_copy(src, slots.at[0], recv_sem).start()

    def give_back(sent, landing, send_sem, recv_sem):
        for m in range(8):
            dst = landing.at[pl.ds(mine, Q)]
            if m:
                remote(sent.at[m], dst, send_sem, recv_sem, group[m]).start()
            else:
                pltpu.make_async_copy(sent.at[0], dst, recv_sem).start()

    for i in range(U):
        src = x_ref.at[pl.ds(aligned(at_a[i] + q * H), H)]
        remote(src, z1.at[i], z1s.at[i], z1r.at[i], pair).start()
    for i in range(U):
        exchange(x_ref, at_b[i], yb.at[i], ybs.at[i], ybr.at[i])

    g_oo, g_ox = coefs(gates, 3, q, q), coefs(gates, 3, q, 1 - q)
    g_xx, g_xo = coefs(gates, 3, 1 - q, 1 - q), coefs(gates, 3, 1 - q, q)

    def both(ref, first, count):
        return tuple(ref[pl.ds(first + part, count, stride=2), :] for part in range(2))

    def task(name, i):
        u = UNITS[i][0]
        if name == "m":
            pltpu.make_async_copy(joined_hbm, joined, jsem).wait()
            build_local(joined, order_ref, total, high, low)
        elif name == "a1":
            wait_for(ao.at[i], aosem.at[i])
            wait_for(z1.at[i], z1r.at[i])
            step = 64
            for first in range(0, H, 2 * step):
                own, partner = both(ao.at[i], first, step), both(z1.at[i], first, step)
                to_other = cmul_add(g_xx, partner, g_xo, own)
                to_own = cmul_add(g_oo, own, g_ox, partner)
                for part in range(2):
                    g1[i, 0, pl.ds(first + part, step, stride=2), :] = to_other[part]
                    g1[i, 1, pl.ds(first + part, step, stride=2), :] = to_own[part]
            remote(g1.at[i], f1.at[i], f1s.at[i], f1r.at[i], beyond).start()
        elif name == "a2":
            wait_for(f1.at[i], f1r.at[i])
            remote(f1.at[i], f2.at[i], f2s.at[i], f2r.at[i], pair).start()
        elif name == "a3":
            wait_for(f2.at[i], f2r.at[i])
            remote(f2.at[i, 1], f3.at[i], f3s.at[i, 1], f3r.at[i, 1], beyond).start()
            dst = an.at[i, pl.ds(high_half, H)]
            remote(f2.at[i, 0], dst, f3s.at[i, 0], f3r.at[i, 0], beyond).start()
        elif name == "a4":
            wait_for(f3.at[i], f3r.at[i, 1])
            dst = an.at[i, pl.ds(low_half, H)]
            remote(f3.at[i], dst, f4s.at[i], f4r.at[i], pair).start()
        elif name == "a5":
            wait_for(an.at[i, pl.ds(low_half, H)], f3r.at[i, 0])
            wait_for(an.at[i, pl.ds(high_half, H)], f4r.at[i])
            exchange(an.at[i], 0, ya.at[i], yas.at[i], yar.at[i])
        elif name == "a6":
            wait_for(ya.at[i], yar.at[i])
            group_step(ya.at[i], sa.at[i], gates, parities, high, low)
            give_back(sa.at[i], (ta if u else oa).at[i], tas.at[i], tar.at[i])
        elif name == "a7":
            landed = (ta if u else oa).at[i]
            wait_for(landed, tar.at[i])
            if u:
                remote(landed, oa.at[i], oas.at[i], oar.at[i], across[u]).start()
            else:
                pltpu.make_async_copy(landed, out_ref.at[pl.ds(at_a[i], R)], outsem).start()
        elif name == "a8":
            wait_for(oa.at[i], oar.at[i])
            pltpu.make_async_copy(oa.at[i], out_ref.at[pl.ds(at_a[i], R)], outsem).start()
        elif name == "b1":
            wait_for(yb.at[i], ybr.at[i])
            group_step(yb.at[i], sb.at[i], gates, parities, high, low)
            give_back(sb.at[i], (tb if u else ob).at[i], tbs.at[i], tbr.at[i])
        elif name == "b2":
            landed = (tb if u else ob).at[i]
            wait_for(landed, tbr.at[i])
            if u:
                remote(landed, ob.at[i], obs.at[i], obr.at[i], across[u]).start()
        elif name == "bz":
            if u:
                wait_for(ob.at[i], obr.at[i])
            remote(ob.at[i], zb.at[i], zbs.at[i], zbr.at[i], pair).start()
        elif name == "b4":
            wait_for(zb.at[i], zbr.at[i])
            step = 64
            for first in range(0, R, 2 * step):
                own, partner = both(ob.at[i], first, step), both(zb.at[i], first, step)
                mixed = cmul_add(g_oo, own, g_ox, partner)
                for part in range(2):
                    rb[i, pl.ds(first + part, step, stride=2), :] = mixed[part]
            pltpu.make_async_copy(rb.at[i], out_ref.at[pl.ds(at_b[i], R)], outsem).start()

    for name, i in ORDER:
        task(name, i)

    for i in range(U):
        wait_for(z1.at[i], z1s.at[i])
        wait_for(f1.at[i], f1s.at[i])
        wait_for(f2.at[i], f2s.at[i])
        wait_for(f3.at[i], f3s.at[i, 0])
        wait_for(f3.at[i], f3s.at[i, 1])
        wait_for(f3.at[i], f4s.at[i])
        wait_for(ya.at[i, pl.ds(1, 7)], yas.at[i])
        wait_for(sa.at[i, pl.ds(1, 7)], tas.at[i])
        wait_for(yb.at[i, pl.ds(1, 7)], ybs.at[i])
        wait_for(sb.at[i, pl.ds(1, 7)], tbs.at[i])
        wait_for(zb.at[i], zbs.at[i])
        if UNITS[i][0]:
            wait_for(oa.at[i], oas.at[i])
            wait_for(ob.at[i], obs.at[i])
    wait_for(out_ref, outsem)


def body(amplitudes, joined_gates, qubit_order, global_gates):
    rows = amplitudes.shape[1] // LANES
    mixed = amplitudes.reshape(2, rows, LANES).transpose(1, 0, 2).reshape(2 * rows, LANES)
    f32 = jnp.float32
    vmem = lambda *shape: pltpu.VMEM(shape + (LANES,), f32)
    dma = lambda *shape: pltpu.SemaphoreType.DMA(shape)
    out = pl.pallas_call(
        kernel,
        out_shape=jax.ShapeDtypeStruct((2 * rows, LANES), f32),
        in_specs=[
            pl.BlockSpec(memory_space=pl.ANY),
            pl.BlockSpec(memory_space=pl.ANY),
            pl.BlockSpec(memory_space=pltpu.SMEM),
            pl.BlockSpec(memory_space=pltpu.SMEM),
        ],
        out_specs=pl.BlockSpec(memory_space=pl.ANY),
        scratch_shapes=[
            pltpu.VMEM(joined_gates.shape, f32),
            pltpu.VMEM((512, 256), f32),
            pltpu.VMEM((512, 512), jnp.bfloat16),
            pltpu.VMEM((512, 512), jnp.bfloat16),
            vmem(U, H), vmem(U, H), vmem(U, 2, H), vmem(U, 2, H), vmem(U, 2, H), vmem(U, H), vmem(U, R),
            vmem(U, 8, Q), vmem(U, 8, Q), vmem(U, R), vmem(U, R),
            vmem(U, 8, Q), vmem(U, 8, Q), vmem(U, R), vmem(U, R), vmem(U, R), vmem(U, R),
            pltpu.SemaphoreType.DMA, dma(U), pltpu.SemaphoreType.DMA,
            dma(U), dma(U), dma(U), dma(U), dma(U), dma(U), dma(U, 2), dma(U, 2), dma(U), dma(U),
            dma(U), dma(U), dma(U), dma(U), dma(U), dma(U),
            dma(U), dma(U), dma(U), dma(U), dma(U), dma(U), dma(U), dma(U),
        ],
        compiler_params=pltpu.CompilerParams(
            collective_id=0, has_side_effects=True, vmem_limit_bytes=48 * 2**20
        ),
        name="circuit",
    )(mixed, joined_gates, qubit_order, global_gates)
    return out.reshape(rows, 2, LANES).transpose(1, 0, 2).reshape(2, rows * LANES)


def solution(mesh):
    in_specs = (P(None, ("wide", "narrow")), P(), P(), P())
    out_specs = P(None, ("wide", "narrow"))
    return jax.shard_map(body, mesh=mesh, in_specs=in_specs, out_specs=out_specs, check_vma=False)
```

profile of v0, /device:TPU:1, one launch (start us, length us, event | category | flops | bytes accessed | tf_op | source)
XLA Modules:
  0.0 91.9 jit_solution(1130546049871045912)
XLA Ops:
  0.0 0.8 copy.6.gates
  0.8 0.0 copy-start
  0.8 1.6 %copy-done = f32[2,262144]{1,0:T(2,128)S(1)} copy-done((f32[2,262144]{1,0:T(2,128)S(1)}, f32[2,262144]{1,0:T(2,128)}, u32[]{:S(2)}) %copy-start) | copy-done | bytes 2097176
  2.4 0.0 copy-start.1
  2.4 1.0 %copy-done.1 = f32[4,2,128,128]{3,2,1,0:T(8,128)S(1)} copy-done((f32[4,2,128,128]{3,2,1,0:T(8,128)S(1)}, f32[4,2,128,128]{3,2,1,0:T(8,128)}, u32[]{:S(2)}) %copy-start.1) | copy-done | bytes 524312
  3.4 0.0 copy-start.2
  3.4 0.7 copy-done.2
  4.1 86.5 %circuit.1 = f32[4096,128]{1,0:T(8,128)S(1)} custom-call(f32[4096,128]{1,0:T(8,128)S(1)} %bitcast.11, f32[4,2,128,128]{3,2,1,0:T(8,128)S(1)} %copy-done.1, s32[4,8]{1,0:T(4,128)S(1)} %copy-done.2, f32[4,2,2,2]{3,2,1,0:T(2,128)S(1)} %copy.6.gates), custom_call_target="tpu_custom_call" | custom-call | tf_op jit(solution)/shard_map/circuit/pallas_call | solution.py:288
  90.6 1.3 %copy.9 = f32[2,262144]{1,0:T(2,128)} copy(f32[2,262144]{1,0:T(2,128)S(1)} %bitcast.10) | data formatting | bytes 4194304
Async XLA Ops:
  0.8 1.6 %copy-start = (f32[2,262144]{1,0:T(2,128)S(1)}, f32[2,262144]{1,0:T(2,128)}, u32[]{:S(2)}) copy-start(f32[2,262144]{1,0:T(2,128)} %param.4) | copy-start | bytes 6291460
  2.4 1.0 %copy-start.1 = (f32[4,2,128,128]{3,2,1,0:T(8,128)S(1)}, f32[4,2,128,128]{3,2,1,0:T(8,128)}, u32[]{:S(2)}) copy-start(f32[4,2,128,128]{3,2,1,0:T(8,128)} %joined_hbm.1) | copy-start | bytes 1572868
  3.4 0.7 copy-start.2
where the time goes:
time: 92.2 us; the launch traced here: 91.9 us
  Pallas kernels  86.5 us (94%)
  local copies, waits for them, and re-layouts  5.43 us (6%)
    pallas_call x1, Pallas kernels, body(): pl.pallas_call(kernel, out_shape=jax.ShapeDtypeStruct((2 * rows, LANES),...  86.5 us
    unnamed x8, local copies, waits for them, and re-layouts  5.43 us

commit v1 on v0

--- a/solution.py
+++ b/solution.py
@@ -11,14 +11,19 @@
 LANES = 128
 BLOCK = 512
 
-UNITS = ((1, 0), (3, 0), (2, 0), (0, 0))
+UNITS = ((2, 0), (2, 1), (1, 0), (1, 1), (3, 0), (3, 1), (0, 0), (0, 1))
 ORDER = (
-    ("m", -1), ("a1", 0), ("b1", 0), ("a1", 1), ("b1", 1), ("a1", 2), ("b1", 2), ("a2", 0), ("a1", 3),
-    ("b1", 3), ("b2", 0), ("a2", 1), ("b2", 1), ("a3", 0), ("b2", 2), ("a2", 2), ("b2", 3), ("a3", 1),
-    ("a2", 3), ("a3", 2), ("a4", 0), ("a3", 3), ("bz", 0), ("a5", 0), ("a4", 1), ("a6", 0), ("a4", 2),
-    ("b4", 0), ("a5", 1), ("bz", 1), ("a7", 0), ("a5", 2), ("a4", 3), ("a6", 1), ("a6", 2), ("a8", 0),
-    ("bz", 2), ("b4", 1), ("a5", 3), ("a7", 1), ("a7", 2), ("bz", 3), ("a6", 3), ("a8", 1), ("b4", 2),
-    ("b4", 3), ("a7", 3), ("a8", 2),
+    ("m0", -1), ("m1", -1), ("a1", 0), ("a1", 1), ("m2", -1), ("a1", 2), ("m3", -1), ("a1", 3), ("a1", 4),
+    ("b1", 0), ("a2", 0), ("b1", 1), ("a1", 5), ("b1", 2), ("a1", 6), ("b1", 3), ("a2", 1), ("b1", 4),
+    ("a1", 7), ("b1", 5), ("b1", 6), ("b1", 7), ("a3", 0), ("b2", 0), ("a2", 2), ("b2", 1), ("a2", 3),
+    ("b2", 2), ("a3", 1), ("b2", 3), ("a2", 4), ("b2", 4), ("a3", 2), ("b2", 5), ("a2", 5), ("b2", 6),
+    ("a3", 3), ("b2", 7), ("a2", 6), ("a3", 4), ("a2", 7), ("a3", 5), ("a4", 0), ("a3", 6), ("bz", 0),
+    ("a4", 1), ("a3", 7), ("a5", 0), ("a4", 2), ("bz", 1), ("b4", 0), ("a4", 3), ("a5", 1), ("a6", 0),
+    ("a5", 2), ("a4", 4), ("bz", 2), ("b4", 1), ("a4", 5), ("a6", 1), ("a5", 3), ("a7", 0), ("a5", 4),
+    ("a4", 6), ("a6", 2), ("bz", 3), ("b4", 2), ("a4", 7), ("a7", 1), ("a5", 5), ("a6", 3), ("a5", 6),
+    ("a8", 0), ("bz", 4), ("a6", 4), ("a7", 2), ("b4", 3), ("bz", 5), ("a6", 5), ("a5", 7), ("a8", 1),
+    ("a7", 3), ("bz", 6), ("a6", 6), ("b4", 4), ("a8", 2), ("a7", 4), ("bz", 7), ("a7", 5), ("b4", 5),
+    ("a8", 3), ("a6", 7), ("a7", 6), ("b4", 6), ("a8", 4), ("b4", 7), ("a8", 5), ("a7", 7),
 )
 
 
@@ -45,7 +50,7 @@
 
 
 def coefs(gates, layer, row, col):
-    return gates[layer, 0, row, col], gates[layer, 1, row, col]
+    return gates[0, row, col, layer], gates[1, row, col, layer]
 
 
 def exact_dot(a, b, dims):
@@ -54,29 +59,30 @@
     )
 
 
-def build_local(joined, order, total, high, low):
-    layers = joined.shape[0]
+def build_layer(joined, order, total, layer):
     rows = lax.broadcasted_iota(jnp.int32, (256, 256), 0)
     cols = lax.broadcasted_iota(jnp.int32, (256, 256), 1)
-    eye = (rows == cols).astype(jnp.float32)
-    total[pl.ds(0, 256), :] = eye
-    total[pl.ds(256, 256), :] = jnp.zeros((256, 256), jnp.float32)
-    for layer in range(layers):
-        parts = []
-        for half in range(2):
-            old = total[:, pl.ds(half * LANES, LANES)]
-            by_real = exact_dot(old, joined[layer, 0], ((1,), (1,)))
-            by_imag = exact_dot(old, joined[layer, 1], ((1,), (1,)))
-            real = by_real[:256] - by_imag[256:]
-            imag = by_imag[:256] + by_real[256:]
-            parts.append(jnp.concatenate([real, imag], axis=0))
-        mixed = jnp.concatenate(parts, axis=1)
-        source = jnp.zeros((256, 256), jnp.int32)
-        for qubit in range(8):
-            bit = jnp.bitwise_and(jnp.right_shift(cols, qubit), 1)
-            source = source + jnp.left_shift(bit, order[layer, qubit])
-        picker = (rows == source).astype(jnp.float32)
-        total[...] = exact_dot(mixed, picker, ((1,), (0,)))
+    if layer == 0:
+        total[pl.ds(0, 256), :] = (rows == cols).astype(jnp.float32)
+        total[pl.ds(256, 256), :] = jnp.zeros((256, 256), jnp.float32)
+    parts = []
+    for half in range(2):
+        old = total[:, pl.ds(half * LANES, LANES)]
+        by_real = exact_dot(old, joined[layer, 0], ((1,), (1,)))
+        by_imag = exact_dot(old, joined[layer, 1], ((1,), (1,)))
+        real = by_real[:256] - by_imag[256:]
+        imag = by_imag[:256] + by_real[256:]
+        parts.append(jnp.concatenate([real, imag], axis=0))
+    mixed = jnp.concatenate(parts, axis=1)
+    source = jnp.zeros((256, 256), jnp.int32)
+    for qubit in range(8):
+        bit = jnp.bitwise_and(jnp.right_shift(cols, qubit), 1)
+        source = source + jnp.left_shift(bit, order[layer, qubit])
+    picker = (rows == source).astype(jnp.float32)
+    total[...] = exact_dot(mixed, picker, ((1,), (0,)))
+
+
+def split_local(total, high, low):
     for half in range(2):
         for half_out in range(2):
             real = total[pl.ds(half * LANES, LANES), pl.ds(half_out * LANES, LANES)]
@@ -119,10 +125,10 @@
 
 
 def kernel(
-    x_ref, joined_hbm, order_ref, gates, out_ref,
-    joined, total, high, low,
+    x_ref, joined_hbm, order_hbm, gates_hbm, out_ref,
+    joined, order, gates, total, high, low,
     ao, z1, g1, f1, f2, f3, an, ya, sa, ta, oa, yb, sb, tb, ob, zb, rb,
-    jsem, aosem, outsem,
+    jsem, osem, gsem, aosem, outsem,
     z1s, z1r, f1s, f1r, f2s, f2r, f3s, f3r, f4s, f4r,
     yas, yar, tas, tar, oas, oar, ybs, ybr, tbs, tbr, obs, obr, zbs, zbr,
 ):
@@ -147,7 +153,6 @@
     for there in partners:
         pl.semaphore_signal(barrier, inc=1, device_id=there, device_id_type=MESH)
 
-    pltpu.make_async_copy(joined_hbm, joined, jsem).start()
     for i in range(U):
         pltpu.make_async_copy(x_ref.at[pl.ds(aligned(at_a[i] + (1 - q) * H), H)], ao.at[i], aosem.at[i]).start()
     pl.semaphore_wait(barrier, len(partners))
@@ -176,12 +181,16 @@
             else:
                 pltpu.make_async_copy(sent.at[0], dst, recv_sem).start()
 
+    pltpu.make_async_copy(gates_hbm, gates, gsem).start()
+    pltpu.make_async_copy(order_hbm, order, osem).start()
     for i in range(U):
         src = x_ref.at[pl.ds(aligned(at_a[i] + q * H), H)]
         remote(src, z1.at[i], z1s.at[i], z1r.at[i], pair).start()
     for i in range(U):
         exchange(x_ref, at_b[i], yb.at[i], ybs.at[i], ybr.at[i])
 
+    pltpu.make_async_copy(joined_hbm, joined, jsem).start()
+    pltpu.make_async_copy(gates_hbm, gates, gsem).wait()
     g_oo, g_ox = coefs(gates, 3, q, q), coefs(gates, 3, q, 1 - q)
     g_xx, g_xo = coefs(gates, 3, 1 - q, 1 - q), coefs(gates, 3, 1 - q, q)
 
@@ -190,13 +199,18 @@
 
     def task(name, i):
         u = UNITS[i][0]
-        if name == "m":
-            pltpu.make_async_copy(joined_hbm, joined, jsem).wait()
-            build_local(joined, order_ref, total, high, low)
+        if name[0] == "m":
+            layer = int(name[1])
+            if layer == 0:
+                pltpu.make_async_copy(joined_hbm, joined, jsem).wait()
+                pltpu.make_async_copy(order_hbm, order, osem).wait()
+            build_layer(joined, order, total, layer)
+            if layer == joined.shape[0] - 1:
+                split_local(total, high, low)
         elif name == "a1":
             wait_for(ao.at[i], aosem.at[i])
             wait_for(z1.at[i], z1r.at[i])
-            step = 64
+            step = min(64, H // 2)
             for first in range(0, H, 2 * step):
                 own, partner = both(ao.at[i], first, step), both(z1.at[i], first, step)
                 to_other = cmul_add(g_xx, partner, g_xo, own)
@@ -282,6 +296,7 @@
 def body(amplitudes, joined_gates, qubit_order, global_gates):
     rows = amplitudes.shape[1] // LANES
     mixed = amplitudes.reshape(2, rows, LANES).transpose(1, 0, 2).reshape(2 * rows, LANES)
+    gates = global_gates.transpose(1, 2, 3, 0)
     f32 = jnp.float32
     vmem = lambda *shape: pltpu.VMEM(shape + (LANES,), f32)
     dma = lambda *shape: pltpu.SemaphoreType.DMA(shape)
@@ -289,30 +304,32 @@
         kernel,
         out_shape=jax.ShapeDtypeStruct((2 * rows, LANES), f32),
         in_specs=[
-            pl.BlockSpec(memory_space=pl.ANY),
-            pl.BlockSpec(memory_space=pl.ANY),
-            pl.BlockSpec(memory_space=pltpu.SMEM),
-            pl.BlockSpec(memory_space=pltpu.SMEM),
+            pl.BlockSpec(memory_space=pltpu.HBM),
+            pl.BlockSpec(memory_space=pltpu.HBM),
+            pl.BlockSpec(memory_space=pltpu.HBM),
+            pl.BlockSpec(memory_space=pltpu.HBM),
         ],
         out_specs=pl.BlockSpec(memory_space=pl.ANY),
         scratch_shapes=[
             pltpu.VMEM(joined_gates.shape, f32),
+            pltpu.SMEM(qubit_order.shape, jnp.int32),
+            pltpu.SMEM(gates.shape, f32),
             pltpu.VMEM((512, 256), f32),
             pltpu.VMEM((512, 512), jnp.bfloat16),
             pltpu.VMEM((512, 512), jnp.bfloat16),
             vmem(U, H), vmem(U, H), vmem(U, 2, H), vmem(U, 2, H), vmem(U, 2, H), vmem(U, H), vmem(U, R),
             vmem(U, 8, Q), vmem(U, 8, Q), vmem(U, R), vmem(U, R),
             vmem(U, 8, Q), vmem(U, 8, Q), vmem(U, R), vmem(U, R), vmem(U, R), vmem(U, R),
-            pltpu.SemaphoreType.DMA, dma(U), pltpu.SemaphoreType.DMA,
+            pltpu.SemaphoreType.DMA, pltpu.SemaphoreType.DMA, pltpu.SemaphoreType.DMA, dma(U), pltpu.SemaphoreType.DMA,
             dma(U), dma(U), dma(U), dma(U), dma(U), dma(U), dma(U, 2), dma(U, 2), dma(U), dma(U),
             dma(U), dma(U), dma(U), dma(U), dma(U), dma(U),
             dma(U), dma(U), dma(U), dma(U), dma(U), dma(U), dma(U), dma(U),
         ],
         compiler_params=pltpu.CompilerParams(
-            collective_id=0, has_side_effects=True, vmem_limit_bytes=48 * 2**20
+            collective_id=0, has_side_effects=True, vmem_limit_bytes=62 * 2**20
         ),
         name="circuit",
-    )(mixed, joined_gates, qubit_order, global_gates)
+    )(mixed, joined_gates, qubit_order, gates)
     return out.reshape(rows, 2, LANES).transpose(1, 0, 2).reshape(2, rows * LANES)
 
 

time: 92.2 us -> 83 us (0.900)
  Pallas kernels: 86.5 us -> 80.2 us
  local copies, waits for them, and re-layouts: 5.43 us -> 2.61 us
    pallas_call x1, Pallas kernels: 86.5 us -> 80.2 us  [body(): pl.pallas_call(kernel, out_shape=jax.ShapeDtypeStruct((2 * rows, LANES),...]
    unnamed x8 -> x1, local copies, waits for them, and re-layouts: 5.43 us -> 2.61 us
where the time goes in v1:
time: 83 us; the launch traced here: 82.8 us
  Pallas kernels  80.2 us (97%)
  local copies, waits for them, and re-layouts  2.61 us (3%)
    pallas_call x1, Pallas kernels, body(): pl.pallas_call(kernel, out_shape=jax.ShapeDtypeStruct((2 * rows, LANES),...  80.2 us
    unnamed x1, local copies, waits for them, and re-layouts  2.61 us

profile of v1, /device:TPU:1, one launch (start us, length us, event | category | flops | bytes accessed | tf_op | source)
XLA Modules:
  0.0 82.8 jit_solution(14281775316174710130)
XLA Ops:
  0.0 80.2 %circuit.1 = f32[4096,128]{1,0:T(8,128)} custom-call(f32[4096,128]{1,0:T(8,128)} %bitcast.12, f32[4,2,128,128]{3,2,1,0:T(8,128)} %joined_hbm.1, s32[4,8]{1,0:T(4,128)} %order_hbm.1, f32[2,2,2,4]{3,2,1,0:T(2,128)} %bitcast.13), custom_call_target="tpu_custom_call" | custom-call | tf_op jit(solution)/shard_map/circuit/pallas_call | solution.py:303
  80.2 2.6 %copy.8 = f32[2,262144]{1,0:T(2,128)} copy(f32[2,262144]{1,0:T(2,128)} %bitcast.11) | data formatting | bytes 4194304

commit v2 on v1

--- a/solution.py
+++ b/solution.py
@@ -12,18 +12,22 @@
 BLOCK = 512
 
 UNITS = ((2, 0), (2, 1), (1, 0), (1, 1), (3, 0), (3, 1), (0, 0), (0, 1))
+A_LAST = (3, 4, 7)
+B_FIRST = (2, 6, 7)
 ORDER = (
-    ("m0", -1), ("m1", -1), ("a1", 0), ("a1", 1), ("m2", -1), ("a1", 2), ("m3", -1), ("a1", 3), ("a1", 4),
-    ("b1", 0), ("a2", 0), ("b1", 1), ("a1", 5), ("b1", 2), ("a1", 6), ("b1", 3), ("a2", 1), ("b1", 4),
-    ("a1", 7), ("b1", 5), ("b1", 6), ("b1", 7), ("a3", 0), ("b2", 0), ("a2", 2), ("b2", 1), ("a2", 3),
-    ("b2", 2), ("a3", 1), ("b2", 3), ("a2", 4), ("b2", 4), ("a3", 2), ("b2", 5), ("a2", 5), ("b2", 6),
-    ("a3", 3), ("b2", 7), ("a2", 6), ("a3", 4), ("a2", 7), ("a3", 5), ("a4", 0), ("a3", 6), ("bz", 0),
-    ("a4", 1), ("a3", 7), ("a5", 0), ("a4", 2), ("bz", 1), ("b4", 0), ("a4", 3), ("a5", 1), ("a6", 0),
-    ("a5", 2), ("a4", 4), ("bz", 2), ("b4", 1), ("a4", 5), ("a6", 1), ("a5", 3), ("a7", 0), ("a5", 4),
-    ("a4", 6), ("a6", 2), ("bz", 3), ("b4", 2), ("a4", 7), ("a7", 1), ("a5", 5), ("a6", 3), ("a5", 6),
-    ("a8", 0), ("bz", 4), ("a6", 4), ("a7", 2), ("b4", 3), ("bz", 5), ("a6", 5), ("a5", 7), ("a8", 1),
-    ("a7", 3), ("bz", 6), ("a6", 6), ("b4", 4), ("a8", 2), ("a7", 4), ("bz", 7), ("a7", 5), ("b4", 5),
-    ("a8", 3), ("a6", 7), ("a7", 6), ("b4", 6), ("a8", 4), ("b4", 7), ("a8", 5), ("a7", 7),
+    ("a0", 5), ("bz", 2), ("a0", 1), ("a0", 6), ("a0", 2), ("a0", 0), ("ay", 4), ("m0", -1), ("m1", -1),
+    ("a1", 5), ("m2", -1), ("bz", 7), ("b4", 2), ("m3", -1), ("a1", 1), ("a1", 6), ("a6", 4), ("bz", 6),
+    ("a1", 2), ("a2", 5), ("ay", 3), ("a1", 0), ("by", 4), ("b1", 2), ("a2", 1), ("ay", 7), ("b4", 7),
+    ("a7", 4), ("a6", 3), ("a2", 6), ("b4", 6), ("b1", 4), ("b2", 2), ("a2", 2), ("a3", 5), ("a0", 4),
+    ("a6", 7), ("b1", 7), ("a2", 0), ("a3", 1), ("a7", 3), ("by", 1), ("b3", 2), ("b1", 6), ("a4", 5),
+    ("a3", 6), ("b2", 4), ("by", 0), ("a7", 7), ("a0", 7), ("by", 5), ("a0", 3), ("a4", 1), ("b2", 7),
+    ("a3", 2), ("by", 3), ("b1", 1), ("a1", 4), ("b2", 6), ("a4", 6), ("b1", 0), ("a3", 0), ("b1", 5),
+    ("a4", 2), ("a5", 5), ("b1", 3), ("a1", 7), ("bz", 4), ("b2", 1), ("a2", 4), ("a1", 3), ("b2", 0),
+    ("a5", 1), ("b2", 5), ("a4", 0), ("a5", 6), ("a6", 5), ("a5", 2), ("b2", 3), ("a2", 7), ("a6", 1),
+    ("b4", 4), ("a6", 6), ("a2", 3), ("a7", 5), ("a3", 4), ("a6", 2), ("a5", 0), ("bz", 1), ("a7", 1),
+    ("a7", 6), ("a3", 7), ("bz", 0), ("a4", 4), ("a8", 5), ("a7", 2), ("a3", 3), ("a6", 0), ("bz", 5),
+    ("a8", 1), ("a4", 7), ("b4", 1), ("a8", 2), ("a4", 3), ("b4", 0), ("a7", 0), ("a5", 4), ("bz", 3),
+    ("b4", 5), ("a5", 7), ("a5", 3), ("a8", 0), ("b4", 3),
 )
 
 
@@ -127,8 +131,8 @@
 def kernel(
     x_ref, joined_hbm, order_hbm, gates_hbm, out_ref,
     joined, order, gates, total, high, low,
-    ao, z1, g1, f1, f2, f3, an, ya, sa, ta, oa, yb, sb, tb, ob, zb, rb,
-    jsem, osem, gsem, aosem, outsem,
+    ao, z1, g1, f1, f2, f3, an, ya, sa, ta, oa, yb, sb, tb, ob, zb, rb, xb,
+    jsem, osem, gsem, aosem, bosem, outsem,
     z1s, z1r, f1s, f1r, f2s, f2r, f3s, f3r, f4s, f4r,
     yas, yar, tas, tar, oas, oar, ybs, ybr, tbs, tbr, obs, obr, zbs, zbr,
 ):
@@ -153,8 +157,15 @@
     for there in partners:
         pl.semaphore_signal(barrier, inc=1, device_id=there, device_id_type=MESH)
 
+    pltpu.make_async_copy(gates_hbm, gates, gsem).start()
+    pltpu.make_async_copy(order_hbm, order, osem).start()
+    pltpu.make_async_copy(joined_hbm, joined, jsem).start()
     for i in range(U):
-        pltpu.make_async_copy(x_ref.at[pl.ds(aligned(at_a[i] + (1 - q) * H), H)], ao.at[i], aosem.at[i]).start()
+        if i not in A_LAST:
+            src = x_ref.at[pl.ds(aligned(at_a[i] + (1 - q) * H), H)]
+            pltpu.make_async_copy(src, ao.at[i], aosem.at[i]).start()
+        if i in B_FIRST:
+            pltpu.make_async_copy(x_ref.at[pl.ds(at_b[i], R)], ob.at[i], bosem.at[i]).start()
     pl.semaphore_wait(barrier, len(partners))
 
     def remote(src, dst, send_sem, recv_sem, there):
@@ -181,18 +192,12 @@
             else:
                 pltpu.make_async_copy(sent.at[0], dst, recv_sem).start()
 
-    pltpu.make_async_copy(gates_hbm, gates, gsem).start()
-    pltpu.make_async_copy(order_hbm, order, osem).start()
-    for i in range(U):
-        src = x_ref.at[pl.ds(aligned(at_a[i] + q * H), H)]
-        remote(src, z1.at[i], z1s.at[i], z1r.at[i], pair).start()
-    for i in range(U):
-        exchange(x_ref, at_b[i], yb.at[i], ybs.at[i], ybr.at[i])
-
-    pltpu.make_async_copy(joined_hbm, joined, jsem).start()
     pltpu.make_async_copy(gates_hbm, gates, gsem).wait()
     g_oo, g_ox = coefs(gates, 3, q, q), coefs(gates, 3, q, 1 - q)
     g_xx, g_xo = coefs(gates, 3, 1 - q, 1 - q), coefs(gates, 3, 1 - q, q)
+
+    def finish(source, at):
+        pltpu.make_async_copy(source, out_ref.at[pl.ds(at, R)], outsem).start()
 
     def both(ref, first, count):
         return tuple(ref[pl.ds(first + part, count, stride=2), :] for part in range(2))
@@ -207,6 +212,17 @@
             build_layer(joined, order, total, layer)
             if layer == joined.shape[0] - 1:
                 split_local(total, high, low)
+        elif name == "ay":
+            exchange(x_ref, at_a[i], ya.at[i], yas.at[i], yar.at[i])
+        elif name == "a0":
+            if i in A_LAST:
+                if u:
+                    wait_for(oa.at[i], oar.at[i])
+                pltpu.make_async_copy(oa.at[i, pl.ds(high_half, H)], ao.at[i], aosem.at[i]).start()
+                src = oa.at[i, pl.ds(low_half, H)]
+            else:
+                src = x_ref.at[pl.ds(aligned(at_a[i] + q * H), H)]
+            remote(src, z1.at[i], z1s.at[i], z1r.at[i], pair).start()
         elif name == "a1":
             wait_for(ao.at[i], aosem.at[i])
             wait_for(z1.at[i], z1r.at[i])
@@ -234,7 +250,10 @@
         elif name == "a5":
             wait_for(an.at[i, pl.ds(low_half, H)], f3r.at[i, 0])
             wait_for(an.at[i, pl.ds(high_half, H)], f4r.at[i])
-            exchange(an.at[i], 0, ya.at[i], yas.at[i], yar.at[i])
+            if i in A_LAST:
+                finish(an.at[i], at_a[i])
+            else:
+                exchange(an.at[i], 0, ya.at[i], yas.at[i], yar.at[i])
         elif name == "a6":
             wait_for(ya.at[i], yar.at[i])
             group_step(ya.at[i], sa.at[i], gates, parities, high, low)
@@ -244,33 +263,50 @@
             wait_for(landed, tar.at[i])
             if u:
                 remote(landed, oa.at[i], oas.at[i], oar.at[i], across[u]).start()
-            else:
-                pltpu.make_async_copy(landed, out_ref.at[pl.ds(at_a[i], R)], outsem).start()
+            elif i not in A_LAST:
+                finish(landed, at_a[i])
         elif name == "a8":
             wait_for(oa.at[i], oar.at[i])
-            pltpu.make_async_copy(oa.at[i], out_ref.at[pl.ds(at_a[i], R)], outsem).start()
+            finish(oa.at[i], at_a[i])
+        elif name == "by":
+            exchange(x_ref, at_b[i], yb.at[i], ybs.at[i], ybr.at[i])
         elif name == "b1":
             wait_for(yb.at[i], ybr.at[i])
             group_step(yb.at[i], sb.at[i], gates, parities, high, low)
-            give_back(sb.at[i], (tb if u else ob).at[i], tbs.at[i], tbr.at[i])
+            give_back(sb.at[i], (tb if u or i in B_FIRST else ob).at[i], tbs.at[i], tbr.at[i])
         elif name == "b2":
-            landed = (tb if u else ob).at[i]
+            landed = (tb if u or i in B_FIRST else ob).at[i]
             wait_for(landed, tbr.at[i])
             if u:
-                remote(landed, ob.at[i], obs.at[i], obr.at[i], across[u]).start()
+                dst = (xb if i in B_FIRST else ob).at[i]
+                remote(landed, dst, obs.at[i], obr.at[i], across[u]).start()
+            elif i in B_FIRST:
+                finish(landed, at_b[i])
+        elif name == "b3":
+            wait_for(xb.at[i], obr.at[i])
+            finish(xb.at[i], at_b[i])
         elif name == "bz":
-            if u:
-                wait_for(ob.at[i], obr.at[i])
-            remote(ob.at[i], zb.at[i], zbs.at[i], zbr.at[i], pair).start()
+            if i in B_FIRST:
+                src = x_ref.at[pl.ds(at_b[i], R)]
+            else:
+                src = ob.at[i]
+                if u:
+                    wait_for(src, obr.at[i])
+            remote(src, zb.at[i], zbs.at[i], zbr.at[i], pair).start()
         elif name == "b4":
+            if i in B_FIRST:
+                wait_for(ob.at[i], bosem.at[i])
             wait_for(zb.at[i], zbr.at[i])
-            step = 64
+            step = min(64, R // 2)
             for first in range(0, R, 2 * step):
                 own, partner = both(ob.at[i], first, step), both(zb.at[i], first, step)
                 mixed = cmul_add(g_oo, own, g_ox, partner)
                 for part in range(2):
                     rb[i, pl.ds(first + part, step, stride=2), :] = mixed[part]
-            pltpu.make_async_copy(rb.at[i], out_ref.at[pl.ds(at_b[i], R)], outsem).start()
+            if i in B_FIRST:
+                exchange(rb.at[i], 0, yb.at[i], ybs.at[i], ybr.at[i])
+            else:
+                finish(rb.at[i], at_b[i])
 
     for name, i in ORDER:
         task(name, i)
@@ -302,7 +338,7 @@
     dma = lambda *shape: pltpu.SemaphoreType.DMA(shape)
     out = pl.pallas_call(
         kernel,
-        out_shape=jax.ShapeDtypeStruct((2 * rows, LANES), f32),
+        out_shape=pltpu.VMEM((2 * rows, LANES), f32),
         in_specs=[
             pl.BlockSpec(memory_space=pltpu.HBM),
             pl.BlockSpec(memory_space=pltpu.HBM),
@@ -319,17 +355,17 @@
             pltpu.VMEM((512, 512), jnp.bfloat16),
             vmem(U, H), vmem(U, H), vmem(U, 2, H), vmem(U, 2, H), vmem(U, 2, H), vmem(U, H), vmem(U, R),
             vmem(U, 8, Q), vmem(U, 8, Q), vmem(U, R), vmem(U, R),
-            vmem(U, 8, Q), vmem(U, 8, Q), vmem(U, R), vmem(U, R), vmem(U, R), vmem(U, R),
-            pltpu.SemaphoreType.DMA, pltpu.SemaphoreType.DMA, pltpu.SemaphoreType.DMA, dma(U), pltpu.SemaphoreType.DMA,
+            vmem(U, 8, Q), vmem(U, 8, Q), vmem(U, R), vmem(U, R), vmem(U, R), vmem(U, R), vmem(U, R),
+            pltpu.SemaphoreType.DMA, pltpu.SemaphoreType.DMA, pltpu.SemaphoreType.DMA, dma(U), dma(U), pltpu.SemaphoreType.DMA,
             dma(U), dma(U), dma(U), dma(U), dma(U), dma(U), dma(U, 2), dma(U, 2), dma(U), dma(U),
             dma(U), dma(U), dma(U), dma(U), dma(U), dma(U),
             dma(U), dma(U), dma(U), dma(U), dma(U), dma(U), dma(U), dma(U),
         ],
         compiler_params=pltpu.CompilerParams(
-            collective_id=0, has_side_effects=True, vmem_limit_bytes=62 * 2**20
+            collective_id=0, has_side_effects=True, vmem_limit_bytes=48 * 2**20
         ),
         name="circuit",
-    )(mixed, joined_gates, qubit_order, gates)
+    )(*(pltpu.with_memory_space_constraint(v, pltpu.HBM) for v in (mixed, joined_gates, qubit_order, gates)))
     return out.reshape(rows, 2, LANES).transpose(1, 0, 2).reshape(2, rows * LANES)
 
 

time: 83 us -> 78.4 us (0.945)
  Pallas kernels: 80.2 us -> 77 us
  local copies, waits for them, and re-layouts: 2.61 us -> 1.32 us
    pallas_call x1, Pallas kernels: 80.2 us -> 77 us  [body(): pl.pallas_call(kernel, out_shape=pltpu.VMEM((2 * rows, LANES), f32), in_s...]
    unnamed x1, local copies, waits for them, and re-layouts: 2.61 us -> 1.32 us
where the time goes in v2:
time: 78.4 us
  Pallas kernels  77 us (98%)
  local copies, waits for them, and re-layouts  1.32 us (2%)
    pallas_call x1, Pallas kernels, body(): pl.pallas_call(kernel, out_shape=pltpu.VMEM((2 * rows, LANES), f32), in_s...  77 us

profile of v2, /device:TPU:1, one launch (start us, length us, event | category | flops | bytes accessed | tf_op | source)
XLA Modules:
  0.0 78.4 jit_solution(5486602832817730750)
XLA Ops:
  0.0 77.0 %circuit.1 = f32[4096,128]{1,0:T(8,128)S(1)} custom-call(f32[4096,128]{1,0:T(8,128)} %bitcast.12, f32[4,2,128,128]{3,2,1,0:T(8,128)} %joined_hbm.1, s32[4,8]{1,0:T(4,128)} %order_hbm.1, f32[2,2,2,4]{3,2,1,0:T(2,128)} %bitcast.13), custom_call_target="tpu_custom_call" | custom-call | tf_op jit(solution)/shard_map/circuit/pallas_call | solution.py:339
  77.0 1.3 %copy.8 = f32[2,262144]{1,0:T(2,128)} copy(f32[2,262144]{1,0:T(2,128)S(1)} %bitcast.11) | data formatting | bytes 4194304

commit v3 on v2

--- a/solution.py
+++ b/solution.py
@@ -12,22 +12,24 @@
 BLOCK = 512
 
 UNITS = ((2, 0), (2, 1), (1, 0), (1, 1), (3, 0), (3, 1), (0, 0), (0, 1))
-A_LAST = (3, 4, 7)
-B_FIRST = (2, 6, 7)
+A_LAST = (0, 5, 6)
+B_FIRST = (4, 5)
+LEAD = 7
+FIRST = 10
 ORDER = (
-    ("a0", 5), ("bz", 2), ("a0", 1), ("a0", 6), ("a0", 2), ("a0", 0), ("ay", 4), ("m0", -1), ("m1", -1),
-    ("a1", 5), ("m2", -1), ("bz", 7), ("b4", 2), ("m3", -1), ("a1", 1), ("a1", 6), ("a6", 4), ("bz", 6),
-    ("a1", 2), ("a2", 5), ("ay", 3), ("a1", 0), ("by", 4), ("b1", 2), ("a2", 1), ("ay", 7), ("b4", 7),
-    ("a7", 4), ("a6", 3), ("a2", 6), ("b4", 6), ("b1", 4), ("b2", 2), ("a2", 2), ("a3", 5), ("a0", 4),
-    ("a6", 7), ("b1", 7), ("a2", 0), ("a3", 1), ("a7", 3), ("by", 1), ("b3", 2), ("b1", 6), ("a4", 5),
-    ("a3", 6), ("b2", 4), ("by", 0), ("a7", 7), ("a0", 7), ("by", 5), ("a0", 3), ("a4", 1), ("b2", 7),
-    ("a3", 2), ("by", 3), ("b1", 1), ("a1", 4), ("b2", 6), ("a4", 6), ("b1", 0), ("a3", 0), ("b1", 5),
-    ("a4", 2), ("a5", 5), ("b1", 3), ("a1", 7), ("bz", 4), ("b2", 1), ("a2", 4), ("a1", 3), ("b2", 0),
-    ("a5", 1), ("b2", 5), ("a4", 0), ("a5", 6), ("a6", 5), ("a5", 2), ("b2", 3), ("a2", 7), ("a6", 1),
-    ("b4", 4), ("a6", 6), ("a2", 3), ("a7", 5), ("a3", 4), ("a6", 2), ("a5", 0), ("bz", 1), ("a7", 1),
-    ("a7", 6), ("a3", 7), ("bz", 0), ("a4", 4), ("a8", 5), ("a7", 2), ("a3", 3), ("a6", 0), ("bz", 5),
-    ("a8", 1), ("a4", 7), ("b4", 1), ("a8", 2), ("a4", 3), ("b4", 0), ("a7", 0), ("a5", 4), ("bz", 3),
-    ("b4", 5), ("a5", 7), ("a5", 3), ("a8", 0), ("b4", 3),
+    ("a0", 2), ("a0", 7), ("a0", 1), ("a0", 4), ("a0", 3), ("ay", 0), ("ay", 5), ("m0", -1), ("m1", -1),
+    ("bz", 5), ("a1", 2), ("a1", 7), ("m2", -1), ("bz", 4), ("m3", -1), ("a6", 0), ("a1", 1), ("a6", 5),
+    ("a1", 4), ("a2", 2), ("a1", 3), ("ay", 6), ("b4", 5), ("by", 7), ("by", 0), ("by", 1), ("a2", 7),
+    ("by", 6), ("by", 2), ("by", 3), ("b4", 4), ("a7", 0), ("a2", 1), ("a7", 5), ("a3", 2), ("a6", 6),
+    ("a2", 4), ("b1", 5), ("a3", 7), ("b1", 7), ("a2", 3), ("a0", 0), ("b1", 0), ("a0", 5), ("b1", 1),
+    ("a3", 1), ("a4", 2), ("b1", 6), ("b1", 2), ("a3", 4), ("a4", 7), ("b1", 3), ("b1", 4), ("a3", 3),
+    ("a7", 6), ("a4", 1), ("a0", 6), ("a1", 0), ("b2", 5), ("a1", 5), ("b2", 7), ("bz", 7), ("a4", 4),
+    ("a5", 2), ("b2", 0), ("a5", 7), ("b2", 1), ("a4", 3), ("a5", 1), ("b3", 5), ("b2", 6), ("a1", 6),
+    ("b2", 2), ("bz", 6), ("a2", 0), ("b2", 3), ("b4", 7), ("b2", 4), ("a2", 5), ("a5", 4), ("a6", 2),
+    ("a5", 3), ("a6", 7), ("a2", 6), ("a6", 1), ("b4", 6), ("a6", 4), ("a7", 2), ("a3", 0), ("bz", 0),
+    ("a6", 3), ("b3", 4), ("a7", 7), ("a3", 5), ("bz", 1), ("a7", 1), ("a8", 2), ("a7", 4), ("a4", 0),
+    ("a3", 6), ("a7", 3), ("bz", 2), ("a4", 5), ("b4", 0), ("a8", 1), ("a4", 6), ("b4", 1), ("a8", 4),
+    ("a5", 0), ("bz", 3), ("a8", 3), ("b4", 2), ("a5", 5), ("a5", 6), ("b4", 3),
 )
 
 
@@ -37,6 +39,11 @@
 H = R // 2
 Q = R // 8
 NQ = Q // 4
+PIECES = 4
+
+
+def pieces(i):
+    return PIECES if i == ORDER[-1][1] else 1
 
 
 def flip(value, mask, bits):
@@ -132,7 +139,7 @@
     x_ref, joined_hbm, order_hbm, gates_hbm, out_ref,
     joined, order, gates, total, high, low,
     ao, z1, g1, f1, f2, f3, an, ya, sa, ta, oa, yb, sb, tb, ob, zb, rb, xb,
-    jsem, osem, gsem, aosem, bosem, outsem,
+    answer, jsem, osem, gsem, aosem, bosem, outsem,
     z1s, z1r, f1s, f1r, f2s, f2r, f3s, f3r, f4s, f4r,
     yas, yar, tas, tar, oas, oar, ybs, ybr, tbs, tbr, obs, obr, zbs, zbr,
 ):
@@ -153,20 +160,21 @@
     mine = aligned(s * Q)
 
     barrier = pltpu.get_barrier_semaphore()
-    partners = [pair, beyond] + group[1:] + across[1:]
+    partners = [pair] + group[1:] + across[1:]
     for there in partners:
         pl.semaphore_signal(barrier, inc=1, device_id=there, device_id_type=MESH)
 
-    pltpu.make_async_copy(gates_hbm, gates, gsem).start()
-    pltpu.make_async_copy(order_hbm, order, osem).start()
-    pltpu.make_async_copy(joined_hbm, joined, jsem).start()
-    for i in range(U):
-        if i not in A_LAST:
-            src = x_ref.at[pl.ds(aligned(at_a[i] + (1 - q) * H), H)]
-            pltpu.make_async_copy(src, ao.at[i], aosem.at[i]).start()
-        if i in B_FIRST:
-            pltpu.make_async_copy(x_ref.at[pl.ds(at_b[i], R)], ob.at[i], bosem.at[i]).start()
-    pl.semaphore_wait(barrier, len(partners))
+    @pl.when(q == 0)
+    def _():
+        pl.semaphore_signal(barrier, inc=1, device_id=beyond, device_id_type=MESH)
+
+
+    pl.semaphore_wait(barrier, len(partners) + q)
+
+    @pl.when(q == 1)
+    def _():
+        pl.semaphore_signal(answer, inc=1, device_id=beyond, device_id_type=MESH)
+
 
     def remote(src, dst, send_sem, recv_sem, there):
         return pltpu.make_async_remote_copy(
@@ -191,10 +199,6 @@
                 remote(sent.at[m], dst, send_sem, recv_sem, group[m]).start()
             else:
                 pltpu.make_async_copy(sent.at[0], dst, recv_sem).start()
-
-    pltpu.make_async_copy(gates_hbm, gates, gsem).wait()
-    g_oo, g_ox = coefs(gates, 3, q, q), coefs(gates, 3, q, 1 - q)
-    g_xx, g_xo = coefs(gates, 3, 1 - q, 1 - q), coefs(gates, 3, 1 - q, q)
 
     def finish(source, at):
         pltpu.make_async_copy(source, out_ref.at[pl.ds(at, R)], outsem).start()
@@ -213,7 +217,7 @@
             if layer == joined.shape[0] - 1:
                 split_local(total, high, low)
         elif name == "ay":
-            exchange(x_ref, at_a[i], ya.at[i], yas.at[i], yar.at[i])
+            exchange(x_ref, at_a[i], ya.at[i], yas, yar.at[i])
         elif name == "a0":
             if i in A_LAST:
                 if u:
@@ -222,7 +226,7 @@
                 src = oa.at[i, pl.ds(low_half, H)]
             else:
                 src = x_ref.at[pl.ds(aligned(at_a[i] + q * H), H)]
-            remote(src, z1.at[i], z1s.at[i], z1r.at[i], pair).start()
+            remote(src, z1.at[i], z1s, z1r.at[i], pair).start()
         elif name == "a1":
             wait_for(ao.at[i], aosem.at[i])
             wait_for(z1.at[i], z1r.at[i])
@@ -234,52 +238,52 @@
                 for part in range(2):
                     g1[i, 0, pl.ds(first + part, step, stride=2), :] = to_other[part]
                     g1[i, 1, pl.ds(first + part, step, stride=2), :] = to_own[part]
-            remote(g1.at[i], f1.at[i], f1s.at[i], f1r.at[i], beyond).start()
+            remote(g1.at[i], f1.at[i], f1s, f1r.at[i], beyond).start()
         elif name == "a2":
             wait_for(f1.at[i], f1r.at[i])
-            remote(f1.at[i], f2.at[i], f2s.at[i], f2r.at[i], pair).start()
+            remote(f1.at[i], f2.at[i], f2s, f2r.at[i], pair).start()
         elif name == "a3":
             wait_for(f2.at[i], f2r.at[i])
-            remote(f2.at[i, 1], f3.at[i], f3s.at[i, 1], f3r.at[i, 1], beyond).start()
+            remote(f2.at[i, 1], f3.at[i], f3s, f3r.at[i, 1], beyond).start()
             dst = an.at[i, pl.ds(high_half, H)]
-            remote(f2.at[i, 0], dst, f3s.at[i, 0], f3r.at[i, 0], beyond).start()
+            remote(f2.at[i, 0], dst, f3s, f3r.at[i, 0], beyond).start()
         elif name == "a4":
             wait_for(f3.at[i], f3r.at[i, 1])
             dst = an.at[i, pl.ds(low_half, H)]
-            remote(f3.at[i], dst, f4s.at[i], f4r.at[i], pair).start()
+            remote(f3.at[i], dst, f4s, f4r.at[i], pair).start()
         elif name == "a5":
             wait_for(an.at[i, pl.ds(low_half, H)], f3r.at[i, 0])
             wait_for(an.at[i, pl.ds(high_half, H)], f4r.at[i])
             if i in A_LAST:
                 finish(an.at[i], at_a[i])
             else:
-                exchange(an.at[i], 0, ya.at[i], yas.at[i], yar.at[i])
+                exchange(an.at[i], 0, ya.at[i], yas, yar.at[i])
         elif name == "a6":
             wait_for(ya.at[i], yar.at[i])
             group_step(ya.at[i], sa.at[i], gates, parities, high, low)
-            give_back(sa.at[i], (ta if u else oa).at[i], tas.at[i], tar.at[i])
+            give_back(sa.at[i], (ta if u else oa).at[i], tas, tar.at[i])
         elif name == "a7":
             landed = (ta if u else oa).at[i]
             wait_for(landed, tar.at[i])
             if u:
-                remote(landed, oa.at[i], oas.at[i], oar.at[i], across[u]).start()
+                remote(landed, oa.at[i], oas, oar.at[i], across[u]).start()
             elif i not in A_LAST:
                 finish(landed, at_a[i])
         elif name == "a8":
             wait_for(oa.at[i], oar.at[i])
             finish(oa.at[i], at_a[i])
         elif name == "by":
-            exchange(x_ref, at_b[i], yb.at[i], ybs.at[i], ybr.at[i])
+            exchange(x_ref, at_b[i], yb.at[i], ybs, ybr.at[i])
         elif name == "b1":
             wait_for(yb.at[i], ybr.at[i])
             group_step(yb.at[i], sb.at[i], gates, parities, high, low)
-            give_back(sb.at[i], (tb if u or i in B_FIRST else ob).at[i], tbs.at[i], tbr.at[i])
+            give_back(sb.at[i], (tb if u or i in B_FIRST else ob).at[i], tbs, tbr.at[i])
         elif name == "b2":
             landed = (tb if u or i in B_FIRST else ob).at[i]
             wait_for(landed, tbr.at[i])
             if u:
                 dst = (xb if i in B_FIRST else ob).at[i]
-                remote(landed, dst, obs.at[i], obr.at[i], across[u]).start()
+                remote(landed, dst, obs, obr.at[i], across[u]).start()
             elif i in B_FIRST:
                 finish(landed, at_b[i])
         elif name == "b3":
@@ -292,40 +296,66 @@
                 src = ob.at[i]
                 if u:
                     wait_for(src, obr.at[i])
-            remote(src, zb.at[i], zbs.at[i], zbr.at[i], pair).start()
+            size = R // pieces(i)
+            for j in range(pieces(i)):
+                part = pl.ds(j * size, size)
+                remote(src.at[part], zb.at[i, part], zbs, zbr.at[i, j], pair).start()
         elif name == "b4":
             if i in B_FIRST:
                 wait_for(ob.at[i], bosem.at[i])
-            wait_for(zb.at[i], zbr.at[i])
-            step = min(64, R // 2)
-            for first in range(0, R, 2 * step):
-                own, partner = both(ob.at[i], first, step), both(zb.at[i], first, step)
-                mixed = cmul_add(g_oo, own, g_ox, partner)
-                for part in range(2):
-                    rb[i, pl.ds(first + part, step, stride=2), :] = mixed[part]
+            size = R // pieces(i)
+            step = min(64, size // 2)
+            for j in range(pieces(i)):
+                wait_for(zb.at[i, pl.ds(j * size, size)], zbr.at[i, j])
+                for first in range(j * size, j * size + size, 2 * step):
+                    own, partner = both(ob.at[i], first, step), both(zb.at[i], first, step)
+                    mixed = cmul_add(g_oo, own, g_ox, partner)
+                    for part in range(2):
+                        rb[i, pl.ds(first + part, step, stride=2), :] = mixed[part]
+                if i not in B_FIRST:
+                    dst = out_ref.at[pl.ds(aligned(at_b[i] + j * size), size)]
+                    pltpu.make_async_copy(rb.at[i, pl.ds(j * size, size)], dst, outsem).start()
             if i in B_FIRST:
-                exchange(rb.at[i], 0, yb.at[i], ybs.at[i], ybr.at[i])
-            else:
-                finish(rb.at[i], at_b[i])
-
-    for name, i in ORDER:
+                exchange(rb.at[i], 0, yb.at[i], ybs, ybr.at[i])
+
+    for name, i in ORDER[:LEAD]:
         task(name, i)
-
+    pltpu.make_async_copy(gates_hbm, gates, gsem).start()
+    pltpu.make_async_copy(order_hbm, order, osem).start()
+    pltpu.make_async_copy(joined_hbm, joined, jsem).start()
     for i in range(U):
-        wait_for(z1.at[i], z1s.at[i])
-        wait_for(f1.at[i], f1s.at[i])
-        wait_for(f2.at[i], f2s.at[i])
-        wait_for(f3.at[i], f3s.at[i, 0])
-        wait_for(f3.at[i], f3s.at[i, 1])
-        wait_for(f3.at[i], f4s.at[i])
-        wait_for(ya.at[i, pl.ds(1, 7)], yas.at[i])
-        wait_for(sa.at[i, pl.ds(1, 7)], tas.at[i])
-        wait_for(yb.at[i, pl.ds(1, 7)], ybs.at[i])
-        wait_for(sb.at[i, pl.ds(1, 7)], tbs.at[i])
-        wait_for(zb.at[i], zbs.at[i])
-        if UNITS[i][0]:
-            wait_for(oa.at[i], oas.at[i])
-            wait_for(ob.at[i], obs.at[i])
+        if i not in A_LAST:
+            src = x_ref.at[pl.ds(aligned(at_a[i] + (1 - q) * H), H)]
+            pltpu.make_async_copy(src, ao.at[i], aosem.at[i]).start()
+        if i in B_FIRST:
+            pltpu.make_async_copy(x_ref.at[pl.ds(at_b[i], R)], ob.at[i], bosem.at[i]).start()
+    pltpu.make_async_copy(gates_hbm, gates, gsem).wait()
+    g_oo, g_ox = coefs(gates, 3, q, q), coefs(gates, 3, q, 1 - q)
+    g_xx, g_xo = coefs(gates, 3, 1 - q, 1 - q), coefs(gates, 3, 1 - q, q)
+
+    for name, i in ORDER[LEAD:FIRST]:
+        task(name, i)
+
+    @pl.when(q == 0)
+    def _():
+        pl.semaphore_wait(answer, 1)
+
+    for name, i in ORDER[FIRST:-1]:
+        task(name, i)
+    moved = sum(1 for u, _ in UNITS if u)
+    wait_for(z1, z1s)
+    wait_for(f1, f1s)
+    wait_for(f2, f2s)
+    wait_for(f2, f3s)
+    wait_for(f3, f4s)
+    wait_for(ya.at[:, pl.ds(1, 7)], yas)
+    wait_for(sa.at[:, pl.ds(1, 7)], tas)
+    wait_for(yb.at[:, pl.ds(1, 7)], ybs)
+    wait_for(sb.at[:, pl.ds(1, 7)], tbs)
+    wait_for(oa.at[pl.ds(0, moved)], oas)
+    wait_for(ob.at[pl.ds(0, moved)], obs)
+    wait_for(zb, zbs)
+    task(*ORDER[-1])
     wait_for(out_ref, outsem)
 
 
@@ -335,7 +365,7 @@
     gates = global_gates.transpose(1, 2, 3, 0)
     f32 = jnp.float32
     vmem = lambda *shape: pltpu.VMEM(shape + (LANES,), f32)
-    dma = lambda *shape: pltpu.SemaphoreType.DMA(shape)
+    dma = lambda *shape: pltpu.SemaphoreType.DMA(shape) if shape else pltpu.SemaphoreType.DMA
     out = pl.pallas_call(
         kernel,
         out_shape=pltpu.VMEM((2 * rows, LANES), f32),
@@ -356,10 +386,11 @@
             vmem(U, H), vmem(U, H), vmem(U, 2, H), vmem(U, 2, H), vmem(U, 2, H), vmem(U, H), vmem(U, R),
             vmem(U, 8, Q), vmem(U, 8, Q), vmem(U, R), vmem(U, R),
             vmem(U, 8, Q), vmem(U, 8, Q), vmem(U, R), vmem(U, R), vmem(U, R), vmem(U, R), vmem(U, R),
+            pltpu.SemaphoreType.REGULAR,
             pltpu.SemaphoreType.DMA, pltpu.SemaphoreType.DMA, pltpu.SemaphoreType.DMA, dma(U), dma(U), pltpu.SemaphoreType.DMA,
-            dma(U), dma(U), dma(U), dma(U), dma(U), dma(U), dma(U, 2), dma(U, 2), dma(U), dma(U),
-            dma(U), dma(U), dma(U), dma(U), dma(U), dma(U),
-            dma(U), dma(U), dma(U), dma(U), dma(U), dma(U), dma(U), dma(U),
+            dma(), dma(U), dma(), dma(U), dma(), dma(U), dma(), dma(U, 2), dma(), dma(U),
+            dma(), dma(U), dma(), dma(U), dma(), dma(U),
+            dma(), dma(U), dma(), dma(U), dma(), dma(U), dma(), dma(U, PIECES),
         ],
         compiler_params=pltpu.CompilerParams(
             collective_id=0, has_side_effects=True, vmem_limit_bytes=48 * 2**20

time: 78.4 us -> 77 us (0.982)
  Pallas kernels: 77 us -> 75.6 us
    pallas_call x1, Pallas kernels: 77 us -> 75.6 us  [body(): pl.pallas_call(kernel, out_shape=pltpu.VMEM((2 * rows, LANES), f32), in_s...]
where the time goes in v3:
time: 77 us; the launch traced here: 76.9 us
  Pallas kernels  75.6 us (98%)
  local copies, waits for them, and re-layouts  1.32 us (2%)
    pallas_call x1, Pallas kernels, body(): pl.pallas_call(kernel, out_shape=pltpu.VMEM((2 * rows, LANES), f32), in_s...  75.6 us

profile of v3, /device:TPU:1, one launch (start us, length us, event | category | flops | bytes accessed | tf_op | source)
XLA Modules:
  0.0 76.9 jit_solution(17403808060253760665)
XLA Ops:
  0.0 75.6 %circuit.1 = f32[4096,128]{1,0:T(8,128)S(1)} custom-call(f32[4096,128]{1,0:T(8,128)} %bitcast.12, f32[4,2,128,128]{3,2,1,0:T(8,128)} %joined_hbm.1, s32[4,8]{1,0:T(4,128)} %order_hbm.1, f32[2,2,2,4]{3,2,1,0:T(2,128)} %bitcast.13), custom_call_target="tpu_custom_call" | custom-call | tf_op jit(solution)/shard_map/circuit/pallas_call | solution.py:369
  75.6 1.3 %copy.8 = f32[2,262144]{1,0:T(2,128)} copy(f32[2,262144]{1,0:T(2,128)S(1)} %bitcast.11) | data formatting | bytes 4194304

commit v4 on v3

--- a/solution.py
+++ b/solution.py
@@ -11,25 +11,25 @@
 LANES = 128
 BLOCK = 512
 
-UNITS = ((2, 0), (2, 1), (1, 0), (1, 1), (3, 0), (3, 1), (0, 0), (0, 1))
-A_LAST = (0, 5, 6)
-B_FIRST = (4, 5)
-LEAD = 7
+UNITS = ((0, 0), (0, 1), (1, 0), (1, 1), (2, 0), (2, 1), (3, 0), (3, 1))
+A_LAST = (0, 2, 6)
+B_FIRST = (1, 4, 6, 7)
+LEAD = 6
 FIRST = 10
 ORDER = (
-    ("a0", 2), ("a0", 7), ("a0", 1), ("a0", 4), ("a0", 3), ("ay", 0), ("ay", 5), ("m0", -1), ("m1", -1),
-    ("bz", 5), ("a1", 2), ("a1", 7), ("m2", -1), ("bz", 4), ("m3", -1), ("a6", 0), ("a1", 1), ("a6", 5),
-    ("a1", 4), ("a2", 2), ("a1", 3), ("ay", 6), ("b4", 5), ("by", 7), ("by", 0), ("by", 1), ("a2", 7),
-    ("by", 6), ("by", 2), ("by", 3), ("b4", 4), ("a7", 0), ("a2", 1), ("a7", 5), ("a3", 2), ("a6", 6),
-    ("a2", 4), ("b1", 5), ("a3", 7), ("b1", 7), ("a2", 3), ("a0", 0), ("b1", 0), ("a0", 5), ("b1", 1),
-    ("a3", 1), ("a4", 2), ("b1", 6), ("b1", 2), ("a3", 4), ("a4", 7), ("b1", 3), ("b1", 4), ("a3", 3),
-    ("a7", 6), ("a4", 1), ("a0", 6), ("a1", 0), ("b2", 5), ("a1", 5), ("b2", 7), ("bz", 7), ("a4", 4),
-    ("a5", 2), ("b2", 0), ("a5", 7), ("b2", 1), ("a4", 3), ("a5", 1), ("b3", 5), ("b2", 6), ("a1", 6),
-    ("b2", 2), ("bz", 6), ("a2", 0), ("b2", 3), ("b4", 7), ("b2", 4), ("a2", 5), ("a5", 4), ("a6", 2),
-    ("a5", 3), ("a6", 7), ("a2", 6), ("a6", 1), ("b4", 6), ("a6", 4), ("a7", 2), ("a3", 0), ("bz", 0),
-    ("a6", 3), ("b3", 4), ("a7", 7), ("a3", 5), ("bz", 1), ("a7", 1), ("a8", 2), ("a7", 4), ("a4", 0),
-    ("a3", 6), ("a7", 3), ("bz", 2), ("a4", 5), ("b4", 0), ("a8", 1), ("a4", 6), ("b4", 1), ("a8", 4),
-    ("a5", 0), ("bz", 3), ("a8", 3), ("b4", 2), ("a5", 5), ("a5", 6), ("b4", 3),
+    ("a0", 3), ("bz", 4), ("a0", 4), ("a0", 5), ("a0", 7), ("a0", 1), ("m0", -1), ("m1", -1), ("m2", -1),
+    ("m3", -1), ("ay", 2), ("ay", 0), ("bz", 1), ("ay", 6), ("b4", 4), ("a1", 3), ("bz", 7), ("a1", 4),
+    ("a1", 5), ("by", 0), ("a1", 7), ("by", 3), ("by", 2), ("by", 5), ("a1", 1), ("bz", 6), ("a6", 2),
+    ("b4", 1), ("a2", 3), ("a6", 0), ("a6", 6), ("b4", 7), ("a2", 4), ("b1", 4), ("b1", 0), ("b4", 6),
+    ("a2", 5), ("b1", 3), ("b1", 2), ("a3", 3), ("a2", 7), ("b1", 5), ("a7", 2), ("a3", 4), ("a2", 1),
+    ("b1", 1), ("a7", 0), ("a0", 0), ("a3", 5), ("a4", 3), ("a7", 6), ("a0", 2), ("b1", 7), ("a3", 7),
+    ("a4", 4), ("b2", 4), ("b2", 0), ("a0", 6), ("a3", 1), ("a4", 5), ("b1", 6), ("a1", 0), ("b2", 3),
+    ("a5", 3), ("a4", 7), ("b2", 2), ("b3", 4), ("a1", 2), ("b2", 5), ("bz", 0), ("a5", 4), ("a4", 1),
+    ("b2", 1), ("a1", 6), ("b2", 7), ("a5", 5), ("a2", 0), ("b2", 6), ("a5", 7), ("a6", 3), ("a2", 2),
+    ("a6", 4), ("b4", 0), ("a6", 5), ("a2", 6), ("a5", 1), ("a6", 7), ("b3", 7), ("a7", 3), ("a3", 0),
+    ("bz", 3), ("a7", 4), ("b3", 6), ("a7", 5), ("a3", 2), ("bz", 2), ("a6", 1), ("a8", 3), ("a4", 0),
+    ("a7", 7), ("a3", 6), ("bz", 5), ("a4", 2), ("b4", 3), ("a8", 4), ("a7", 1), ("a4", 6), ("b4", 2),
+    ("a8", 5), ("a5", 0), ("a8", 7), ("b4", 5), ("a5", 2), ("a5", 6),
 )
 
 
@@ -139,7 +139,7 @@
     x_ref, joined_hbm, order_hbm, gates_hbm, out_ref,
     joined, order, gates, total, high, low,
     ao, z1, g1, f1, f2, f3, an, ya, sa, ta, oa, yb, sb, tb, ob, zb, rb, xb,
-    answer, jsem, osem, gsem, aosem, bosem, outsem,
+    near, everyone, jsem, osem, gsem, aosem, bosem, outsem,
     z1s, z1r, f1s, f1r, f2s, f2r, f3s, f3r, f4s, f4r,
     yas, yar, tas, tar, oas, oar, ybs, ybr, tbs, tbr, obs, obr, zbs, zbr,
 ):
@@ -159,22 +159,44 @@
     low_half, high_half = aligned(q * H), aligned((1 - q) * H)
     mine = aligned(s * Q)
 
+    core = lax.rem(s, 2)
+    role = q * 2 + core
+    mate = group[1]
+    crossed = (p * 16 + (1 - q) * 8 + others[1], n)
+    above = ((1 - p) * 16 + q * 8 + s, x * 2 + lax.rem(zh + p, 2))
+    below = ((1 - p) * 16 + q * 8 + s, x * 2 + lax.rem(zh + 1 - p, 2))
+    around = [group[m] for m in (2, 4, 6)] + across[1:] + [above, below]
     barrier = pltpu.get_barrier_semaphore()
-    partners = [pair] + group[1:] + across[1:]
-    for there in partners:
-        pl.semaphore_signal(barrier, inc=1, device_id=there, device_id_type=MESH)
-
-    @pl.when(q == 0)
-    def _():
-        pl.semaphore_signal(barrier, inc=1, device_id=beyond, device_id_type=MESH)
-
-
-    pl.semaphore_wait(barrier, len(partners) + q)
-
-    @pl.when(q == 1)
-    def _():
-        pl.semaphore_signal(answer, inc=1, device_id=beyond, device_id_type=MESH)
-
+
+    def tell(semaphore, there):
+        pl.semaphore_signal(semaphore, inc=1, device_id=there, device_id_type=MESH)
+
+    @pl.when(core == 0)
+    def _():
+        tell(barrier, pair)
+
+    @pl.when(role == 3)
+    def _():
+        tell(barrier, pair)
+        tell(barrier, mate)
+
+    @pl.when(role == 0)
+    def _():
+        pl.semaphore_wait(barrier, 1)
+
+    @pl.when(role == 1)
+    def _():
+        pl.semaphore_wait(barrier, 1)
+        tell(near, pair)
+
+    @pl.when(role == 2)
+    def _():
+        pl.semaphore_wait(barrier, 2)
+        tell(near, mate)
+
+    @pl.when(role == 3)
+    def _():
+        pl.semaphore_wait(near, 2)
 
     def remote(src, dst, send_sem, recv_sem, there):
         return pltpu.make_async_remote_copy(
@@ -320,6 +342,15 @@
 
     for name, i in ORDER[:LEAD]:
         task(name, i)
+
+    @pl.when(role == 3)
+    def _():
+        for there in around:
+            tell(barrier, there)
+        pl.semaphore_wait(barrier, len(around))
+        for there in (mate, pair, crossed):
+            tell(everyone, there)
+
     pltpu.make_async_copy(gates_hbm, gates, gsem).start()
     pltpu.make_async_copy(order_hbm, order, osem).start()
     pltpu.make_async_copy(joined_hbm, joined, jsem).start()
@@ -336,9 +367,9 @@
     for name, i in ORDER[LEAD:FIRST]:
         task(name, i)
 
-    @pl.when(q == 0)
-    def _():
-        pl.semaphore_wait(answer, 1)
+    @pl.when(role < 3)
+    def _():
+        pl.semaphore_wait(everyone, 1)
 
     for name, i in ORDER[FIRST:-1]:
         task(name, i)
@@ -386,7 +417,7 @@
             vmem(U, H), vmem(U, H), vmem(U, 2, H), vmem(U, 2, H), vmem(U, 2, H), vmem(U, H), vmem(U, R),
             vmem(U, 8, Q), vmem(U, 8, Q), vmem(U, R), vmem(U, R),
             vmem(U, 8, Q), vmem(U, 8, Q), vmem(U, R), vmem(U, R), vmem(U, R), vmem(U, R), vmem(U, R),
-            pltpu.SemaphoreType.REGULAR,
+            pltpu.SemaphoreType.REGULAR, pltpu.SemaphoreType.REGULAR,
             pltpu.SemaphoreType.DMA, pltpu.SemaphoreType.DMA, pltpu.SemaphoreType.DMA, dma(U), dma(U), pltpu.SemaphoreType.DMA,
             dma(), dma(U), dma(), dma(U), dma(), dma(U), dma(), dma(U, 2), dma(), dma(U),
             dma(), dma(U), dma(), dma(U), dma(), dma(U),

time: 77 us -> 75.9 us (0.986)
  Pallas kernels: 75.6 us -> 74.5 us
    pallas_call x1, Pallas kernels: 75.6 us -> 74.5 us  [body(): pl.pallas_call(kernel, out_shape=pltpu.VMEM((2 * rows, LANES), f32), in_s...]
where the time goes in v4:
time: 75.9 us; the launch traced here: 75.8 us
  Pallas kernels  74.5 us (98%)
  local copies, waits for them, and re-layouts  1.32 us (2%)
    pallas_call x1, Pallas kernels, body(): pl.pallas_call(kernel, out_shape=pltpu.VMEM((2 * rows, LANES), f32), in_s...  74.5 us

profile of v4, /device:TPU:1, one launch (start us, length us, event | category | flops | bytes accessed | tf_op | source)
XLA Modules:
  0.0 75.8 jit_solution(1328411862274998252)
XLA Ops:
  0.0 74.5 %circuit.1 = f32[4096,128]{1,0:T(8,128)S(1)} custom-call(f32[4096,128]{1,0:T(8,128)} %bitcast.12, f32[4,2,128,128]{3,2,1,0:T(8,128)} %joined_hbm.1, s32[4,8]{1,0:T(4,128)} %order_hbm.1, f32[2,2,2,4]{3,2,1,0:T(2,128)} %bitcast.13), custom_call_target="tpu_custom_call" | custom-call | tf_op jit(solution)/shard_map/circuit/pallas_call | solution.py:400
  74.5 1.3 %copy.8 = f32[2,262144]{1,0:T(2,128)} copy(f32[2,262144]{1,0:T(2,128)S(1)} %bitcast.11) | data formatting | bytes 4194304

commit v5 on v4

--- a/solution.py
+++ b/solution.py
@@ -105,12 +105,12 @@
                 low[at] = (block - top.astype(jnp.float32)).astype(jnp.bfloat16)
 
 
-def group_step(slots, sent, gates, parities, high, low):
+def group_step(slots, sent, start, gates, parities, high, low):
     planes = [None] * 4
     for half in range(2):
         values = []
         for m in range(8):
-            values.append(tuple(slots[m, pl.ds(2 * half + part, NQ, stride=4), :] for part in range(2)))
+            values.append(tuple(slots[pl.ds(start + m * Q + 2 * half + part, NQ, stride=4), :] for part in range(2)))
         for bit in range(3):
             own = parities[bit]
             other = 1 - own
@@ -132,7 +132,7 @@
     result = dot(top, high[...]) + (dot(rest, high[...]) + dot(top, low[...]))
     for m in range(8):
         for k in range(4):
-            sent[m, pl.ds(k, NQ, stride=4), :] = result[m * NQ : (m + 1) * NQ, k * LANES : (k + 1) * LANES]
+            sent[pl.ds(start + m * Q + k, NQ, stride=4), :] = result[m * NQ : (m + 1) * NQ, k * LANES : (k + 1) * LANES]
 
 
 def kernel(
@@ -198,6 +198,9 @@
     def _():
         pl.semaphore_wait(near, 2)
 
+    def unit(ref, i, size=R):
+        return ref.at[pl.ds(i * size, size)]
+
     def remote(src, dst, send_sem, recv_sem, there):
         return pltpu.make_async_remote_copy(
             src_ref=src, dst_ref=dst, send_sem=send_sem, recv_sem=recv_sem, device_id=there, device_id_type=MESH
@@ -206,21 +209,23 @@
     def wait_for(ref, sem):
         pltpu.make_async_copy(ref, ref, sem).wait()
 
-    def exchange(source, base, slots, send_sem, recv_sem):
+    def exchange(source, base, slots, i, send_sem, recv_sem):
         for m in range(8):
             src = source.at[pl.ds(aligned(base + others[m] * Q), Q)]
+            slot = slots.at[pl.ds(i * R + m * Q, Q)]
             if m:
-                remote(src, slots.at[m], send_sem, recv_sem, group[m]).start()
+                remote(src, slot, send_sem, recv_sem, group[m]).start()
             else:
-                pltpu.make_async_copy(src, slots.at[0], recv_sem).start()
-
-    def give_back(sent, landing, send_sem, recv_sem):
+                pltpu.make_async_copy(src, slot, recv_sem).start()
+
+    def give_back(sent, i, landing, send_sem, recv_sem):
         for m in range(8):
             dst = landing.at[pl.ds(mine, Q)]
+            src = sent.at[pl.ds(i * R + m * Q, Q)]
             if m:
-                remote(sent.at[m], dst, send_sem, recv_sem, group[m]).start()
+                remote(src, dst, send_sem, recv_sem, group[m]).start()
             else:
-                pltpu.make_async_copy(sent.at[0], dst, recv_sem).start()
+                pltpu.make_async_copy(src, dst, recv_sem).start()
 
     def finish(source, at):
         pltpu.make_async_copy(source, out_ref.at[pl.ds(at, R)], outsem).start()
@@ -239,36 +244,36 @@
             if layer == joined.shape[0] - 1:
                 split_local(total, high, low)
         elif name == "ay":
-            exchange(x_ref, at_a[i], ya.at[i], yas, yar.at[i])
+            exchange(x_ref, at_a[i], ya, i, yas, yar.at[i])
         elif name == "a0":
             if i in A_LAST:
                 if u:
                     wait_for(oa.at[i], oar.at[i])
-                pltpu.make_async_copy(oa.at[i, pl.ds(high_half, H)], ao.at[i], aosem.at[i]).start()
+                pltpu.make_async_copy(oa.at[i, pl.ds(high_half, H)], unit(ao, i, H), aosem.at[i]).start()
                 src = oa.at[i, pl.ds(low_half, H)]
             else:
                 src = x_ref.at[pl.ds(aligned(at_a[i] + q * H), H)]
-            remote(src, z1.at[i], z1s, z1r.at[i], pair).start()
+            remote(src, unit(z1, i, H), z1s, z1r.at[i], pair).start()
         elif name == "a1":
-            wait_for(ao.at[i], aosem.at[i])
-            wait_for(z1.at[i], z1r.at[i])
+            wait_for(unit(ao, i, H), aosem.at[i])
+            wait_for(unit(z1, i, H), z1r.at[i])
             step = min(64, H // 2)
             for first in range(0, H, 2 * step):
-                own, partner = both(ao.at[i], first, step), both(z1.at[i], first, step)
+                own, partner = both(ao, i * H + first, step), both(z1, i * H + first, step)
                 to_other = cmul_add(g_xx, partner, g_xo, own)
                 to_own = cmul_add(g_oo, own, g_ox, partner)
                 for part in range(2):
-                    g1[i, 0, pl.ds(first + part, step, stride=2), :] = to_other[part]
-                    g1[i, 1, pl.ds(first + part, step, stride=2), :] = to_own[part]
-            remote(g1.at[i], f1.at[i], f1s, f1r.at[i], beyond).start()
+                    g1[pl.ds(i * R + first + part, step, stride=2), :] = to_other[part]
+                    g1[pl.ds(i * R + H + first + part, step, stride=2), :] = to_own[part]
+            remote(unit(g1, i), unit(f1, i), f1s, f1r.at[i], beyond).start()
         elif name == "a2":
-            wait_for(f1.at[i], f1r.at[i])
-            remote(f1.at[i], f2.at[i], f2s, f2r.at[i], pair).start()
+            wait_for(unit(f1, i), f1r.at[i])
+            remote(unit(f1, i), unit(f2, i), f2s, f2r.at[i], pair).start()
         elif name == "a3":
-            wait_for(f2.at[i], f2r.at[i])
-            remote(f2.at[i, 1], f3.at[i], f3s, f3r.at[i, 1], beyond).start()
+            wait_for(unit(f2, i), f2r.at[i])
+            remote(f2.at[pl.ds(i * R + H, H)], f3.at[i], f3s, f3r.at[i, 1], beyond).start()
             dst = an.at[i, pl.ds(high_half, H)]
-            remote(f2.at[i, 0], dst, f3s, f3r.at[i, 0], beyond).start()
+            remote(f2.at[pl.ds(i * R, H)], dst, f3s, f3r.at[i, 0], beyond).start()
         elif name == "a4":
             wait_for(f3.at[i], f3r.at[i, 1])
             dst = an.at[i, pl.ds(low_half, H)]
@@ -279,11 +284,11 @@
             if i in A_LAST:
                 finish(an.at[i], at_a[i])
             else:
-                exchange(an.at[i], 0, ya.at[i], yas, yar.at[i])
+                exchange(an.at[i], 0, ya, i, yas, yar.at[i])
         elif name == "a6":
-            wait_for(ya.at[i], yar.at[i])
-            group_step(ya.at[i], sa.at[i], gates, parities, high, low)
-            give_back(sa.at[i], (ta if u else oa).at[i], tas, tar.at[i])
+            wait_for(unit(ya, i), yar.at[i])
+            group_step(ya, sa, i * R, gates, parities, high, low)
+            give_back(sa, i, (ta if u else oa).at[i], tas, tar.at[i])
         elif name == "a7":
             landed = (ta if u else oa).at[i]
             wait_for(landed, tar.at[i])
@@ -295,50 +300,50 @@
             wait_for(oa.at[i], oar.at[i])
             finish(oa.at[i], at_a[i])
         elif name == "by":
-            exchange(x_ref, at_b[i], yb.at[i], ybs, ybr.at[i])
+            exchange(x_ref, at_b[i], yb, i, ybs, ybr.at[i])
         elif name == "b1":
-            wait_for(yb.at[i], ybr.at[i])
-            group_step(yb.at[i], sb.at[i], gates, parities, high, low)
-            give_back(sb.at[i], (tb if u or i in B_FIRST else ob).at[i], tbs, tbr.at[i])
+            wait_for(unit(yb, i), ybr.at[i])
+            group_step(yb, sb, i * R, gates, parities, high, low)
+            give_back(sb, i, unit(tb if u or i in B_FIRST else ob, i), tbs, tbr.at[i])
         elif name == "b2":
-            landed = (tb if u or i in B_FIRST else ob).at[i]
+            landed = unit(tb if u or i in B_FIRST else ob, i)
             wait_for(landed, tbr.at[i])
             if u:
-                dst = (xb if i in B_FIRST else ob).at[i]
+                dst = unit(xb if i in B_FIRST else ob, i)
                 remote(landed, dst, obs, obr.at[i], across[u]).start()
             elif i in B_FIRST:
                 finish(landed, at_b[i])
         elif name == "b3":
-            wait_for(xb.at[i], obr.at[i])
-            finish(xb.at[i], at_b[i])
+            wait_for(unit(xb, i), obr.at[i])
+            finish(unit(xb, i), at_b[i])
         elif name == "bz":
             if i in B_FIRST:
                 src = x_ref.at[pl.ds(at_b[i], R)]
             else:
-                src = ob.at[i]
+                src = unit(ob, i)
                 if u:
                     wait_for(src, obr.at[i])
             size = R // pieces(i)
             for j in range(pieces(i)):
-                part = pl.ds(j * size, size)
-                remote(src.at[part], zb.at[i, part], zbs, zbr.at[i, j], pair).start()
+                dst = zb.at[pl.ds(i * R + j * size, size)]
+                remote(src.at[pl.ds(j * size, size)], dst, zbs, zbr.at[i, j], pair).start()
         elif name == "b4":
             if i in B_FIRST:
-                wait_for(ob.at[i], bosem.at[i])
+                wait_for(unit(ob, i), bosem.at[i])
             size = R // pieces(i)
             step = min(64, size // 2)
             for j in range(pieces(i)):
-                wait_for(zb.at[i, pl.ds(j * size, size)], zbr.at[i, j])
+                wait_for(zb.at[pl.ds(i * R + j * size, size)], zbr.at[i, j])
                 for first in range(j * size, j * size + size, 2 * step):
-                    own, partner = both(ob.at[i], first, step), both(zb.at[i], first, step)
+                    own, partner = both(ob, i * R + first, step), both(zb, i * R + first, step)
                     mixed = cmul_add(g_oo, own, g_ox, partner)
                     for part in range(2):
-                        rb[i, pl.ds(first + part, step, stride=2), :] = mixed[part]
+                        rb[pl.ds(i * R + first + part, step, stride=2), :] = mixed[part]
                 if i not in B_FIRST:
                     dst = out_ref.at[pl.ds(aligned(at_b[i] + j * size), size)]
-                    pltpu.make_async_copy(rb.at[i, pl.ds(j * size, size)], dst, outsem).start()
+                    pltpu.make_async_copy(rb.at[pl.ds(i * R + j * size, size)], dst, outsem).start()
             if i in B_FIRST:
-                exchange(rb.at[i], 0, yb.at[i], ybs, ybr.at[i])
+                exchange(unit(rb, i), 0, yb, i, ybs, ybr.at[i])
 
     for name, i in ORDER[:LEAD]:
         task(name, i)
@@ -357,9 +362,9 @@
     for i in range(U):
         if i not in A_LAST:
             src = x_ref.at[pl.ds(aligned(at_a[i] + (1 - q) * H), H)]
-            pltpu.make_async_copy(src, ao.at[i], aosem.at[i]).start()
+            pltpu.make_async_copy(src, unit(ao, i, H), aosem.at[i]).start()
         if i in B_FIRST:
-            pltpu.make_async_copy(x_ref.at[pl.ds(at_b[i], R)], ob.at[i], bosem.at[i]).start()
+            pltpu.make_async_copy(x_ref.at[pl.ds(at_b[i], R)], unit(ob, i), bosem.at[i]).start()
     pltpu.make_async_copy(gates_hbm, gates, gsem).wait()
     g_oo, g_ox = coefs(gates, 3, q, q), coefs(gates, 3, q, 1 - q)
     g_xx, g_xo = coefs(gates, 3, 1 - q, 1 - q), coefs(gates, 3, 1 - q, q)
@@ -374,18 +379,18 @@
     for name, i in ORDER[FIRST:-1]:
         task(name, i)
     moved = sum(1 for u, _ in UNITS if u)
-    wait_for(z1, z1s)
-    wait_for(f1, f1s)
-    wait_for(f2, f2s)
-    wait_for(f2, f3s)
+    wait_for(z1.at[pl.ds(0, U * H)], z1s)
+    wait_for(f1.at[pl.ds(0, U * R)], f1s)
+    wait_for(f2.at[pl.ds(0, U * R)], f2s)
+    wait_for(f2.at[pl.ds(0, U * R)], f3s)
     wait_for(f3, f4s)
-    wait_for(ya.at[:, pl.ds(1, 7)], yas)
-    wait_for(sa.at[:, pl.ds(1, 7)], tas)
-    wait_for(yb.at[:, pl.ds(1, 7)], ybs)
-    wait_for(sb.at[:, pl.ds(1, 7)], tbs)
+    wait_for(ya.at[pl.ds(0, U * 7 * Q)], yas)
+    wait_for(sa.at[pl.ds(0, U * 7 * Q)], tas)
+    wait_for(yb.at[pl.ds(0, U * 7 * Q)], ybs)
+    wait_for(sb.at[pl.ds(0, U * 7 * Q)], tbs)
     wait_for(oa.at[pl.ds(0, moved)], oas)
-    wait_for(ob.at[pl.ds(0, moved)], obs)
-    wait_for(zb, zbs)
+    wait_for(ob.at[pl.ds(0, moved * R)], obs)
+    wait_for(zb.at[pl.ds(0, U * R)], zbs)
     task(*ORDER[-1])
     wait_for(out_ref, outsem)
 
@@ -396,6 +401,7 @@
     gates = global_gates.transpose(1, 2, 3, 0)
     f32 = jnp.float32
     vmem = lambda *shape: pltpu.VMEM(shape + (LANES,), f32)
+    whole, half = vmem(U * R + 8), vmem(U * H + 8)
     dma = lambda *shape: pltpu.SemaphoreType.DMA(shape) if shape else pltpu.SemaphoreType.DMA
     out = pl.pallas_call(
         kernel,
@@ -414,9 +420,9 @@
             pltpu.VMEM((512, 256), f32),
             pltpu.VMEM((512, 512), jnp.bfloat16),
             pltpu.VMEM((512, 512), jnp.bfloat16),
-            vmem(U, H), vmem(U, H), vmem(U, 2, H), vmem(U, 2, H), vmem(U, 2, H), vmem(U, H), vmem(U, R),
-            vmem(U, 8, Q), vmem(U, 8, Q), vmem(U, R), vmem(U, R),
-            vmem(U, 8, Q), vmem(U, 8, Q), vmem(U, R), vmem(U, R), vmem(U, R), vmem(U, R), vmem(U, R),
+            half, half, whole, whole, whole, vmem(U, H), vmem(U, R),
+            whole, whole, vmem(U, R), vmem(U, R),
+            whole, whole, whole, whole, whole, whole, whole,
             pltpu.SemaphoreType.REGULAR, pltpu.SemaphoreType.REGULAR,
             pltpu.SemaphoreType.DMA, pltpu.SemaphoreType.DMA, pltpu.SemaphoreType.DMA, dma(U), dma(U), pltpu.SemaphoreType.DMA,
             dma(), dma(U), dma(), dma(U), dma(), dma(U), dma(), dma(U, 2), dma(), dma(U),

time: 75.9 us -> 75.9 us (level)
  no operation moved by 1% of the time
where the time goes in v5:
time: 75.9 us; the launch traced here: 75.8 us
  Pallas kernels  74.5 us (98%)
  local copies, waits for them, and re-layouts  1.32 us (2%)
    pallas_call x1, Pallas kernels, body(): pl.pallas_call(kernel, out_shape=pltpu.VMEM((2 * rows, LANES), f32), in_s...  74.5 us

profile of v5, /device:TPU:1, one launch (start us, length us, event | category | flops | bytes accessed | tf_op | source)
XLA Modules:
  0.0 75.8 jit_solution(6829816819606257799)
XLA Ops:
  0.0 74.5 %circuit.1 = f32[4096,128]{1,0:T(8,128)S(1)} custom-call(f32[4096,128]{1,0:T(8,128)} %bitcast.12, f32[4,2,128,128]{3,2,1,0:T(8,128)} %joined_hbm.1, s32[4,8]{1,0:T(4,128)} %order_hbm.1, f32[2,2,2,4]{3,2,1,0:T(2,128)} %bitcast.13), custom_call_target="tpu_custom_call" | custom-call | tf_op jit(solution)/shard_map/circuit/pallas_call | solution.py:406
  74.5 1.3 %copy.8 = f32[2,262144]{1,0:T(2,128)} copy(f32[2,262144]{1,0:T(2,128)S(1)} %bitcast.11) | data formatting | bytes 4194304

commit v6 on v5

--- a/solution.py
+++ b/solution.py
@@ -145,9 +145,26 @@
 ):
     w, n = lax.axis_index("wide"), lax.axis_index("narrow")
     p, q, s = lax.div(w, 16), lax.rem(lax.div(w, 8), 2), lax.rem(w, 8)
+    core = lax.rem(s, 2)
+    role = q * 2 + core
+    pair = (p * 16 + (1 - q) * 8 + s, n)
+    mate = (w + 1 - 2 * core, n)
+    barrier = pltpu.get_barrier_semaphore()
+
+    def tell(semaphore, there):
+        pl.semaphore_signal(semaphore, inc=1, device_id=there, device_id_type=MESH)
+
+    @pl.when(core == 0)
+    def _():
+        tell(barrier, pair)
+
+    @pl.when(role == 3)
+    def _():
+        tell(barrier, pair)
+        tell(barrier, mate)
+
     x, zh = lax.div(n, 2), lax.rem(n, 2)
     parities = [lax.rem(lax.div(s, 2**bit), 2) for bit in range(3)]
-    pair = (p * 16 + (1 - q) * 8 + s, n)
     same = 1 - lax.rem(p + q, 2)
     beyond = ((1 - p) * 16 + (1 - q) * 8 + s, x * 2 + lax.rem(zh + same, 2))
     others = [flip(s, m, 3) for m in range(8)]
@@ -159,26 +176,10 @@
     low_half, high_half = aligned(q * H), aligned((1 - q) * H)
     mine = aligned(s * Q)
 
-    core = lax.rem(s, 2)
-    role = q * 2 + core
-    mate = group[1]
     crossed = (p * 16 + (1 - q) * 8 + others[1], n)
     above = ((1 - p) * 16 + q * 8 + s, x * 2 + lax.rem(zh + p, 2))
     below = ((1 - p) * 16 + q * 8 + s, x * 2 + lax.rem(zh + 1 - p, 2))
     around = [group[m] for m in (2, 4, 6)] + across[1:] + [above, below]
-    barrier = pltpu.get_barrier_semaphore()
-
-    def tell(semaphore, there):
-        pl.semaphore_signal(semaphore, inc=1, device_id=there, device_id_type=MESH)
-
-    @pl.when(core == 0)
-    def _():
-        tell(barrier, pair)
-
-    @pl.when(role == 3)
-    def _():
-        tell(barrier, pair)
-        tell(barrier, mate)
 
     @pl.when(role == 0)
     def _():
@@ -228,7 +229,7 @@
                 pltpu.make_async_copy(src, dst, recv_sem).start()
 
     def finish(source, at):
-        pltpu.make_async_copy(source, out_ref.at[pl.ds(at, R)], outsem).start()
+        pltpu.make_async_copy(source, out_ref.at[pl.ds(at, source.shape[0])], outsem).start()
 
     def both(ref, first, count):
         return tuple(ref[pl.ds(first + part, count, stride=2), :] for part in range(2))
@@ -279,10 +280,13 @@
             dst = an.at[i, pl.ds(low_half, H)]
             remote(f3.at[i], dst, f4s, f4r.at[i], pair).start()
         elif name == "a5":
-            wait_for(an.at[i, pl.ds(low_half, H)], f3r.at[i, 0])
-            wait_for(an.at[i, pl.ds(high_half, H)], f4r.at[i])
+            first, second = an.at[i, pl.ds(low_half, H)], an.at[i, pl.ds(high_half, H)]
+            wait_for(first, f3r.at[i, 0])
             if i in A_LAST:
-                finish(an.at[i], at_a[i])
+                finish(first, aligned(at_a[i] + low_half))
+            wait_for(second, f4r.at[i])
+            if i in A_LAST:
+                finish(second, aligned(at_a[i] + high_half))
             else:
                 exchange(an.at[i], 0, ya, i, yas, yar.at[i])
         elif name == "a6":

time: 75.9 us -> 75.9 us (level)
  no operation moved by 1% of the time
where the time goes in v6:
time: 75.9 us; the launch traced here: 75.7 us
  Pallas kernels  74.4 us (98%)
  local copies, waits for them, and re-layouts  1.32 us (2%)
    pallas_call x1, Pallas kernels, body(): pl.pallas_call(kernel, out_shape=pltpu.VMEM((2 * rows, LANES), f32), in_s...  74.4 us

profile of v6, /device:TPU:1, one launch (start us, length us, event | category | flops | bytes accessed | tf_op | source)
XLA Modules:
  0.0 75.7 jit_solution(7306548960705075349)
XLA Ops:
  0.0 74.4 %circuit.1 = f32[4096,128]{1,0:T(8,128)S(1)} custom-call(f32[4096,128]{1,0:T(8,128)} %bitcast.12, f32[4,2,128,128]{3,2,1,0:T(8,128)} %joined_hbm.1, s32[4,8]{1,0:T(4,128)} %order_hbm.1, f32[2,2,2,4]{3,2,1,0:T(2,128)} %bitcast.13), custom_call_target="tpu_custom_call" | custom-call | tf_op jit(solution)/shard_map/circuit/pallas_call | solution.py:410
  74.4 1.3 %copy.8 = f32[2,262144]{1,0:T(2,128)} copy(f32[2,262144]{1,0:T(2,128)S(1)} %bitcast.11) | data formatting | bytes 4194304

commit v7 on v5

--- a/solution.py
+++ b/solution.py
@@ -39,7 +39,7 @@
 H = R // 2
 Q = R // 8
 NQ = Q // 4
-PIECES = 4
+PIECES = 1
 
 
 def pieces(i):

time: 75.9 us -> 75.7 us (level)
  no operation moved by 1% of the time
where the time goes in v7:
time: 75.7 us; the launch traced here: 75.6 us
  Pallas kernels  74.3 us (98%)
  local copies, waits for them, and re-layouts  1.32 us (2%)
    pallas_call x1, Pallas kernels, body(): pl.pallas_call(kernel, out_shape=pltpu.VMEM((2 * rows, LANES), f32), in_s...  74.3 us

profile of v7, /device:TPU:1, one launch (start us, length us, event | category | flops | bytes accessed | tf_op | source)
XLA Modules:
  0.0 75.6 jit_solution(576954666487337138)
XLA Ops:
  0.0 74.3 %circuit.1 = f32[4096,128]{1,0:T(8,128)S(1)} custom-call(f32[4096,128]{1,0:T(8,128)} %bitcast.12, f32[4,2,128,128]{3,2,1,0:T(8,128)} %joined_hbm.1, s32[4,8]{1,0:T(4,128)} %order_hbm.1, f32[2,2,2,4]{3,2,1,0:T(2,128)} %bitcast.13), custom_call_target="tpu_custom_call" | custom-call | tf_op jit(solution)/shard_map/circuit/pallas_call | solution.py:406
  74.3 1.3 %copy.8 = f32[2,262144]{1,0:T(2,128)} copy(f32[2,262144]{1,0:T(2,128)S(1)} %bitcast.11) | data formatting | bytes 4194304
